TPU v7x, 512 devices: a whole 4x8x8 slice. The times are simulated.
512 devices in a mesh: cam: 64 (over y, x, core), pt: 8 (over z).
Axes of the slice: x: 4, y: 8, z: 8, core: 2. Of those that a mesh axis runs over, the one named last changes fastest.
Arguments:
- solution: float32 [9, 16384], P(None, 'cam'), may hold values from -0.3125 to 0.3125
- residual: float32 [9, 16384], P(None, 'cam'), may hold values from -6 to 6
- direction: float32 [9, 16384], P(None, 'cam'), may hold values from -6 to 6
- cam_damping: float32 [9, 16384], P(None, 'cam'), may hold values from 4 to 40
- precond: float32 [81, 16384], P(None, 'cam'), may hold values from -0.07 to 3, as said below
- pt_damping: float32 [1048576], P(('cam', 'pt')), may hold values from 0.5 to 2
- cam_jac: float32 [32768, 18, 128], P(('cam', 'pt')), may hold values from -2 to 2
- pt_jac: float32 [32768, 6, 128], P(('cam', 'pt')), may hold values from -6 to 6
- cam_ids: int32 [32768, 128], P(('cam', 'pt')), may hold values from 0 to 255
- point_ids: int32 [32768, 128], P(('cam', 'pt')), may hold values from 0 to 2047
- owners: int32 [32768, 1], P(('cam', 'pt')), may hold values from 0 to 63; in each aligned block of 64 rows (0 to 63, 64 to 127, ...) at most 2 rows name the same one
- valid_counts: int32 [32768], P(('cam', 'pt')), may hold values from 32 to 128, as said below
Outputs:
- new_solution: float32 [9, 16384], P(None, 'cam')
- new_residual: float32 [9, 16384], P(None, 'cam')
- new_direction: float32 [9, 16384], P(None, 'cam')
Inputs may be any that keep to these rules, and one draw needn't show every extreme that they name: `owners`: among the 64 tiles of one device no owner appears more than 2 times. `valid_counts`: every eighth tile is full. `precond`: each 9x9 block is symmetric with a positive, strictly dominant diagonal.
All inputs are finite; a program needn't handle non-finite values.
Results may differ from a plain program's by a relative error of at most 0.0003.
Values sent between devices are 32-bit elements; how exact they have to be, the bound alone decides.
No kernel may reach another device: no remote copies, remote signals or barrier semaphores. Data moves between devices by JAX's collectives and lax.ppermute only.
A program may use at most 64 MiB of HBM per device.

v0:
```python
import jax
import jax.numpy as jnp
from jax import lax
from jax.sharding import PartitionSpec as P


def project(cam_jac, gathered, valid):
    first = jnp.sum(cam_jac[:, 0:9] * gathered, axis=1)
    second = jnp.sum(cam_jac[:, 9:18] * gathered, axis=1)
    return jnp.stack([first, second], axis=1) * valid[:, None, :]


def point_terms(jacobian, errors):
    return jnp.stack(
        [
            jacobian[:, column] * errors[:, 0] + jacobian[:, 3 + column] * errors[:, 1]
            for column in range(3)
        ],
        axis=1,
    )


def normal_terms(jacobian):
    pairs = [(0, 0), (0, 1), (0, 2), (1, 1), (1, 2), (2, 2)]
    return jnp.stack(
        [
            jacobian[:, first] * jacobian[:, second]
            + jacobian[:, 3 + first] * jacobian[:, 3 + second]
            for first, second in pairs
        ],
        axis=1,
    )


def solve_points(rhs, normal, damping):
    upper_aa = normal[0] + damping
    upper_ab = normal[1]
    upper_ac = normal[2]
    upper_bb = normal[3] + damping
    upper_bc = normal[4]
    upper_cc = normal[5] + damping
    minor_aa = upper_bb * upper_cc - upper_bc * upper_bc
    minor_ab = upper_ac * upper_bc - upper_ab * upper_cc
    minor_ac = upper_ab * upper_bc - upper_ac * upper_bb
    minor_bb = upper_aa * upper_cc - upper_ac * upper_ac
    minor_bc = upper_ab * upper_ac - upper_aa * upper_bc
    minor_cc = upper_aa * upper_bb - upper_ab * upper_ab
    determ = upper_aa * minor_aa + upper_ab * minor_ab + upper_ac * minor_ac
    first = (minor_aa * rhs[0] + minor_ab * rhs[1] + minor_ac * rhs[2]) / determ
    second = (minor_ab * rhs[0] + minor_bb * rhs[1] + minor_bc * rhs[2]) / determ
    third = (minor_ac * rhs[0] + minor_bc * rhs[1] + minor_cc * rhs[2]) / determ
    return jnp.stack([first, second, third], axis=0)


def apply_points(jacobian, values):
    return jnp.stack(
        [
            sum((jacobian[:, 3 * row + column] * values[:, column] for column in range(3)))
            for row in range(2)
        ],
        axis=1,
    )


def camera_terms(cam_jac, errors):
    return jnp.stack(
        [
            cam_jac[:, column] * errors[:, 0] + cam_jac[:, 9 + column] * errors[:, 1]
            for column in range(9)
        ],
        axis=1,
    )


def precondition(precond, vector):
    return jnp.sum(precond.reshape(9, 9, -1) * vector[None], axis=1)


def body(
    solution,
    residual,
    direction,
    cam_damping,
    precond,
    pt_damping,
    cam_jac,
    pt_jac,
    cam_ids,
    point_ids,
    owners,
    valid_counts,
):
    owner_count = lax.axis_size("cam")
    tile_count = owners.shape[0]
    tile_width = cam_ids.shape[1]
    per_owner = max(2, 2 * tile_count // owner_count)
    slot_total = owner_count * per_owner
    owner_list = owners[:, 0]
    hits_table = (owner_list[:, None] == jnp.arange(owner_count, dtype=jnp.int32)[None, :]).astype(
        jnp.int32
    )
    slot_rank = jnp.sum((jnp.cumsum(hits_table, axis=0) - 1) * hits_table, axis=1)
    slot_index = owner_list * per_owner + slot_rank
    first_z = precondition(precond, residual)
    local_rz = jnp.sum(residual * first_z)
    product_rz = lax.psum(local_rz, "cam")
    valid = (jnp.arange(tile_width, dtype=jnp.int32)[None, :] < valid_counts[:, None]).astype(
        jnp.float32
    )
    gathered = jnp.take(direction, cam_ids, axis=1).transpose(1, 0, 2)
    errors = project(cam_jac, gathered, valid)
    masked_jac = pt_jac * valid[:, None, :]
    point_float = point_ids.astype(jnp.float32)[:, None, :]
    payload = jnp.concatenate([masked_jac, point_terms(masked_jac, errors), point_float], axis=1)
    outgoing = (
        jnp.zeros((slot_total, payload.shape[1], tile_width), jnp.float32)
        .at[slot_index]
        .set(payload)
    )
    received = lax.all_to_all(outgoing, "cam", split_axis=0, concat_axis=0, tiled=True)
    recv_jac = received[:, 0:6]
    recv_ids = received[:, -1].astype(jnp.int32)
    recv_rhs = received[:, 6:9]
    stacked = jnp.concatenate([recv_rhs, normal_terms(recv_jac)], axis=1)
    flat_terms = stacked.transpose(1, 0, 2).reshape(9, -1)
    sums = (
        jnp.zeros((9, pt_damping.shape[0]), jnp.float32).at[:, recv_ids.reshape(-1)].add(flat_terms)
    )
    point_sol = solve_points(sums[:3], sums[3:], pt_damping)
    slot_sol = jnp.take(point_sol, recv_ids, axis=1).transpose(1, 0, 2)
    returned = lax.all_to_all(slot_sol, "cam", split_axis=0, concat_axis=0, tiled=True)
    mine = returned[slot_index]
    projected = apply_points(masked_jac, mine)
    remain = errors - projected
    cam_terms = camera_terms(cam_jac, remain).transpose(1, 0, 2).reshape(9, -1)
    local_image = (
        jnp.zeros((9, direction.shape[1]), jnp.float32).at[:, cam_ids.reshape(-1)].add(cam_terms)
    )
    image = cam_damping * direction + lax.psum(local_image, "pt")
    local_pq = jnp.sum(direction * image)
    product_pq = lax.psum(local_pq, "cam")
    alpha = product_rz / product_pq
    new_solution = solution + alpha * direction
    new_residual = residual - alpha * image
    next_z = precondition(precond, new_residual)
    product_next = lax.psum(jnp.sum(new_residual * next_z), "cam")
    new_direction = next_z + product_next / product_rz * direction
    return (new_solution, new_residual, new_direction)


def solution(mesh):
    return jax.shard_map(
        body,
        mesh=mesh,
        in_specs=(
            P(None, "cam"),
            P(None, "cam"),
            P(None, "cam"),
            P(None, "cam"),
            P(None, "cam"),
            P(("cam", "pt")),
            P(("cam", "pt"), None, None),
            P(("cam", "pt"), None, None),
            P(("cam", "pt"), None),
            P(("cam", "pt"), None),
            P(("cam", "pt"), None),
            P(("cam", "pt")),
        ),
        out_specs=(P(None, "cam"), P(None, "cam"), P(None, "cam")),
        check_vma=False,
    )
```

profile of v0, /device:TPU:1, one launch (start us, length us, event | category | flops | bytes accessed | tf_op | source)
XLA Modules:
  0.0 615.6 jit_solution(11171134279029201128)
XLA Ops:
  0.7 0.8 bitcast_clamp_fusion
  1.5 0.8 compare_and_fusion.1
  3.1 0.8 select_reduce_fusion
  5.3 0.8 copy.149
  6.2 27.7 %gather_fusion = f32[8192,9]{1,0:T(8,128)} fusion(f32[9,256]{0,1:T(8,128)S(1)} %copy.149, s32[8192]{0:T(1024)S(1)} %bitcast_clamp_fusion), kind=kCustom, calls=%fused_computation | custom fusion | bytes 622592 | tf_op jit(solution)/shard_map/jit(_take)/gather | solution.py:110
  33.8 2.9 copy.150
  36.7 1.0 constant_dynamic-update-slice_fusion
  38.1 2.4 scatter_fusion
  40.6 39.4 %all_to_all.10 = f32[128,10,128]{2,1,0:T(8,128)S(1)} all-to-all(f32[128,10,128]{2,1,0:T(8,128)S(1)} %scatter_fusion), channel_id=1, replica_groups=mesh['cam'=64,'pt'=8] {'cam'}, dimensions={0} | all-to-all | bytes 1310720 | tf_op jit(solution)/shard_map/all_to_all | solution.py:120
  80.1 1.2 slice_convert_fusion
  81.3 2.2 concatenate.7
  84.5 4.7 copy.153
  89.2 102.3 %scatter_custom_fusion.1 = f32[9,2048]{0,1:T(8,128)S(1)} fusion(s32[16384]{0:T(1024)S(1)} %bitcast.71, f32[16384,9]{1,0:T(8,128)} %copy.153, f32[]{:T(128)} %constant.17.clone.1), kind=kCustom, calls=%fused_computation.15 | custom fusion | flops 147456 | bytes 74240 | tf_op jit(solution)/shard_map/scatter-add | solution.py:127
  191.6 4.7 slice_reduce_fusion.8
  196.8 54.4 %gather_fusion.1 = f32[16384,3]{1,0:T(8,128)} fusion(f32[3,2048]{0,1:T(8,128)S(1)} %copy.154, s32[16384]{0:T(1024)S(1)} %fusion.5), kind=kCustom, calls=%fused_computation.1 | custom fusion | bytes 458752 | tf_op jit(solution)/shard_map/jit(_take)/gather | solution.py:130
  251.2 5.5 copy.155
  256.8 0.8 select_bitcast_fusion
  257.6 7.2 %all-to-all-start.1 = ((f32[128,3,128]{2,1,0:T(4,128)}), f32[128,3,128]{2,1,0:T(4,128)S(1)}, u32[]{:S(2)}, u32[]{:S(2)}) async-start(f32[128,3,128]{2,1,0:T(4,128)} %select_bitcast_fusion), calls=%async_computation.1 | async-start | bytes 524288 | tf_op jit(solution)/shard_map/all_to_all | solution.py:131
  265.5 12.4 %all-to-all-done.1 = f32[128,3,128]{2,1,0:T(4,128)S(1)} async-done(((f32[128,3,128]{2,1,0:T(4,128)}), f32[128,3,128]{2,1,0:T(4,128)S(1)}, u32[]{:S(2)}, u32[]{:S(2)}) %all-to-all-start.1) | async-done | bytes 196640 | tf_op jit(solution)/shard_map/all_to_all | solution.py:131
  279.2 2.6 copy.159
  281.9 44.3 %scatter_custom_fusion.2 = f32[9,256]{0,1:T(8,128)S(1)} fusion(s32[8192]{0:T(1024)S(1)} %bitcast.72, f32[8192,9]{1,0:T(8,128)} %copy.159, f32[]{:T(128)} %constant.17.clone.1), kind=kCustom, calls=%fused_computation.41 | custom fusion | flops 73728 | bytes 9728 | tf_op jit(solution)/shard_map/scatter-add | solution.py:137
  326.3 28.9 %psum.29 = f32[9,256]{1,0:T(8,128)S(1)} all-reduce(f32[9,256]{1,0:T(8,128)S(1)} %copy.160), channel_id=1, replica_groups=mesh['cam'=64,'pt'=8] {'pt'}, use_global_device_ids=true, to_apply=%region_10.11 | all-reduce | flops 2304 | bytes 18432 | tf_op jit(solution)/shard_map/psum | solution.py:139
  355.8 131.2 %all-reduce = (f32[]{:T(128)}, f32[]{:T(128)}) all-reduce(f32[]{:T(128)} %multiply_reduce_fusion.4, f32[]{:T(128)} %multiply_reduce_fusion.3), channel_id=1, replica_groups=mesh['cam'=64,'pt'=8] {'cam'}, use_global_device_ids=true, to_apply=%region_2.3 | all-reduce | flops 2 | bytes 16 | tf_op jit(solution)/shard_map/psum | solution.py:106
  489.0 124.7 %psum.31 = f32[]{:T(128)} all-reduce(f32[]{:T(128)} %multiply_reduce_fusion.2), channel_id=1, replica_groups=mesh['cam'=64,'pt'=8] {'cam'}, use_global_device_ids=true, to_apply=%region_15.16 | all-reduce | flops 1 | bytes 8 | tf_op jit(solution)/shard_map/psum | solution.py:146
  (68 shorter events, 8.0 us)
Async XLA Ops:
  0.6 37.1 %copy-start = (f32[64,18,128]{2,0,1:T(8,128)S(1)}, f32[64,18,128]{2,0,1:T(8,128)}, u32[]{:S(2)}) copy-start(f32[64,18,128]{2,0,1:T(8,128)} %param.18) | copy-start | bytes 1769476
  0.6 37.2 %copy-start.7 = (s32[64,128]{1,0:T(8,128)S(1)}, s32[64,128]{1,0:T(8,128)}, u32[]{:S(2)}) copy-start(s32[64,128]{1,0:T(8,128)} %param.21) | copy-start | bytes 98308
  84.4 111.9 %copy-start.9 = (f32[2048]{0:T(1024)S(1)}, f32[2048]{0:T(1024)}, u32[]{:S(2)}) copy-start(f32[2048]{0:T(1024)} %param.17) | copy-start | bytes 24580
  196.3 68.5 %copy-start.1 = (s32[64,128]{1,0:T(8,128)S(1)}, s32[64,128]{1,0:T(8,128)}, u32[]{:S(2)}) copy-start(s32[64,128]{1,0:T(8,128)} %param.20) | copy-start | bytes 98308
  196.3 68.5 %copy-start.5 = (f32[81,256]{1,0:T(8,128)S(1)}, f32[81,256]{1,0:T(8,128)}, u32[]{:S(2)}) copy-start(f32[81,256]{1,0:T(8,128)} %param.16) | copy-start | bytes 248836
  196.3 68.6 %copy-start.3 = (f32[9,256]{1,0:T(8,128)S(1)}, f32[9,256]{1,0:T(8,128)}, u32[]{:S(2)}) copy-start(f32[9,256]{1,0:T(8,128)} %param.13) | copy-start | bytes 27652
  251.2 103.9 %copy-start.2 = (f32[9,256]{1,0:T(8,128)S(1)}, f32[9,256]{1,0:T(8,128)}, u32[]{:S(2)}) copy-start(f32[9,256]{1,0:T(8,128)} %param.14) | copy-start | bytes 27652
  251.2 103.9 %copy-start.6 = (f32[9,256]{1,0:T(8,128)S(1)}, f32[9,256]{1,0:T(8,128)}, u32[]{:S(2)}) copy-start(f32[9,256]{1,0:T(8,128)} %param.15) | copy-start | bytes 27652
  251.2 363.8 %copy-start.8 = (f32[9,256]{1,0:T(8,128)S(1)}, f32[9,256]{1,0:T(8,128)}, u32[]{:S(2)}) copy-start(f32[9,256]{1,0:T(8,128)} %param.12) | copy-start | bytes 27652
  257.6 20.4 %all-to-all-start.1 = ((f32[128,3,128]{2,1,0:T(4,128)}), f32[128,3,128]{2,1,0:T(4,128)S(1)}, u32[]{:S(2)}, u32[]{:S(2)}) async-start(f32[128,3,128]{2,1,0:T(4,128)} %select_bitcast_fusion), calls=%async_computation.1 | async-start | bytes 524288 | tf_op jit(solution)/shard_map/all_to_all | solution.py:131
  488.3 127.3 %copy-start.4 = (f32[9,256]{1,0:T(8,128)}, f32[9,256]{1,0:T(8,128)S(1)}, u32[]{:S(2)}) copy-start(f32[9,256]{1,0:T(8,128)S(1)} %multiply_subtract_fusion) | copy-start | bytes 27652
where the time goes:
time: 616 us
  blocking collectives  324 us (53%)
  other arithmetic  157 us (25%)
  local copies, waits for them, and re-layouts  111 us (18%)
  waiting for transfers between devices  12.4 us (2%)
  starting transfers between devices  7.19 us (1%)
    psum x1, blocking collectives, body(): product_rz = lax.psum(local_rz, 'cam')  131 us
    psum x1, blocking collectives, body(): product_next = lax.psum(jnp.sum(new_residual * next_z), 'cam')  125 us
    scatter-add x1, other arithmetic, body(): jnp.zeros((9, pt_damping.shape[0]), jnp.float32).at[:, recv_ids.reshape(-1)]  102 us
    gather x2, local copies, waits for them, and re-layouts, body(): slot_sol = jnp.take(point_sol, recv_ids, axis=1).transpose(1, 0, 2)  60 us
    scatter-add x1, other arithmetic, body(): jnp.zeros((9, direction.shape[1]), jnp.float32).at[:, cam_ids.reshape(-1)]  44.3 us
    all_to_all x1, blocking collectives, body(): lax.all_to_all(outgoing, 'cam', split_axis=0, concat_axis=0, tiled=True)  39.4 us
    gather x2, local copies, waits for them, and re-layouts, body(): gathered = jnp.take(direction, cam_ids, axis=1).transpose(1, 0, 2)  30.6 us
    psum x1, blocking collectives, body(): image = cam_damping * direction + lax.psum(local_image, 'pt')  28.9 us
  transfers between devices with their start and end apart: 1, of which 1 were waited for; matrix products, arithmetic and copies ran while one was open for 0% of the time, Pallas kernels for 0%

commit v1 on v0

v1 whole, which is shorter than its diff:
```python
import functools

import jax
import jax.numpy as jnp
from jax import lax
from jax.experimental import pallas as pl
from jax.experimental.pallas import tpu as pltpu
from jax.sharding import PartitionSpec as P

LANES = 128
PER_OWNER = 2
SLOT_ROWS = 9
TERM_ROWS = 32
GROUP = 8
POINT_LOW = 256
PARTS = 3

f32 = jnp.float32
bf16 = jnp.bfloat16
i32 = jnp.int32


def split(value):
    high = value.astype(bf16).astype(f32)
    rest = value - high
    middle = rest.astype(bf16).astype(f32)
    low = (rest - middle).astype(bf16).astype(f32)
    return high, middle, low


def lookup(table, index):
    return jnp.take_along_axis(table, index, axis=1, mode="promise_in_bounds")


def contract(left, right):
    return lax.dot_general(left, right, (((1,), (1,)), ((), ())), preferred_element_type=f32)


def pack_kernel(
    owners, counts, direction, cam_ids, cam_jac, pt_jac, point_ids, payload, slots, seen, table
):
    tiles, width = cam_ids.shape
    owner_count = seen.shape[0]
    payload[...] = jnp.zeros(payload.shape, f32)

    @pl.loop(0, owner_count)
    def _(index):
        seen[index] = 0

    table[0:9, :] = direction[...]
    table[9:18, :] = direction[...]
    table[18:24, :] = jnp.zeros((6, table.shape[1]), f32)
    tables = [
        [table[8 * g : 8 * g + 8, LANES * c : LANES * (c + 1)] for c in range(2)] for g in range(3)
    ]
    lane = lax.broadcasted_iota(i32, (1, LANES), 1)
    row8 = lax.broadcasted_iota(i32, (8, LANES), 0)

    @pl.loop(0, tiles, unroll=8)
    def _(tile):
        owner = owners[tile]
        rank = seen[owner]
        seen[owner] = rank + 1
        slot = owner * PER_OWNER + rank
        slots[tile] = slot
        base = slot * SLOT_ROWS
        ids = jnp.broadcast_to(cam_ids[pl.ds(tile, 1), :], (8, LANES))
        low = ids & (LANES - 1)
        upper = ids >= LANES
        picked = [
            jnp.where(upper, lookup(tables[g][1], low), lookup(tables[g][0], low)) for g in range(3)
        ]
        first = cam_jac[tile, 0:8, :] * picked[0]
        second = cam_jac[tile, 8:16, :] * picked[1]
        third = cam_jac[tile, 16:18, :] * picked[2][0:2]
        valid = lane < counts[tile]
        err0 = jnp.sum(first + jnp.where(row8 < 1, second, 0.0), axis=0, keepdims=True)
        err1 = jnp.sum(jnp.where(row8 < 1, 0.0, second), axis=0, keepdims=True) + jnp.sum(
            third, axis=0, keepdims=True
        )
        payload[pl.ds(base, 6), :] = jnp.where(valid, pt_jac[tile], 0.0)
        payload[pl.ds(base + 6, 1), :] = jnp.where(valid, err0, 0.0)
        payload[pl.ds(base + 7, 1), :] = jnp.where(valid, err1, 0.0)
        payload[pl.ds(base + 8, 1), :] = point_ids[pl.ds(tile, 1), :].astype(f32)


def solve_points(rhs, normal, damping):
    upper_aa = normal[0] + damping
    upper_ab = normal[1]
    upper_ac = normal[2]
    upper_bb = normal[3] + damping
    upper_bc = normal[4]
    upper_cc = normal[5] + damping
    minor_aa = upper_bb * upper_cc - upper_bc * upper_bc
    minor_ab = upper_ac * upper_bc - upper_ab * upper_cc
    minor_ac = upper_ab * upper_bc - upper_ac * upper_bb
    minor_bb = upper_aa * upper_cc - upper_ac * upper_ac
    minor_bc = upper_ab * upper_ac - upper_aa * upper_bc
    minor_cc = upper_aa * upper_bb - upper_ab * upper_ab
    determ = upper_aa * minor_aa + upper_ab * minor_ab + upper_ac * minor_ac
    return (
        (minor_aa * rhs[0] + minor_ab * rhs[1] + minor_ac * rhs[2]) / determ,
        (minor_ab * rhs[0] + minor_bb * rhs[1] + minor_bc * rhs[2]) / determ,
        (minor_ac * rhs[0] + minor_bc * rhs[1] + minor_cc * rhs[2]) / determ,
    )


def point_kernel(received, damping, remain, terms, left, right, sums, answers):
    slots = remain.shape[0] // 2
    groups = slots // GROUP
    uppers = damping.shape[0]
    rows = GROUP * SLOT_ROWS
    terms[...] = jnp.zeros(terms.shape, f32)
    sums[...] = jnp.zeros(sums.shape, f32)
    low_of_row = lax.broadcasted_iota(i32, (POINT_LOW, LANES), 0).astype(bf16)

    @pl.loop(0, groups)
    def _(group):
        base = group * rows
        jac = [received[pl.ds(base + r, GROUP, stride=SLOT_ROWS), :] for r in range(6)]
        err0 = received[pl.ds(base + 6, GROUP, stride=SLOT_ROWS), :]
        err1 = received[pl.ds(base + 7, GROUP, stride=SLOT_ROWS), :]
        ids = received[pl.ds(base + 8, GROUP, stride=SLOT_ROWS), :].astype(i32)
        upper = (ids // POINT_LOW).astype(f32)
        lower = (ids & (POINT_LOW - 1)).astype(f32)
        values = [jac[a] * err0 + jac[3 + a] * err1 for a in range(3)]
        for a, b in ((0, 0), (0, 1), (0, 2), (1, 1), (1, 2), (2, 2)):
            values.append(jac[a] * jac[b] + jac[3 + a] * jac[3 + b])
        for term, value in enumerate(values):
            for part, piece in enumerate(split(value)):
                terms[pl.ds(part * 9 + term, GROUP, stride=TERM_ROWS), :] = piece
        for s in range(GROUP):
            columns = slice(s * LANES, (s + 1) * LANES)
            block = terms[s * TERM_ROWS : (s + 1) * TERM_ROWS, :].astype(bf16)
            upper_row = jnp.broadcast_to(upper[s : s + 1, :], (TERM_ROWS, LANES)).astype(bf16)
            lower_row = jnp.broadcast_to(lower[s : s + 1, :], (POINT_LOW, LANES)).astype(bf16)
            for h in range(uppers):
                left[h * TERM_ROWS : (h + 1) * TERM_ROWS, columns] = jnp.where(
                    upper_row == jnp.asarray(h, bf16), block, jnp.zeros_like(block)
                )
            right[:, columns] = jnp.where(
                low_of_row == lower_row, jnp.ones((), bf16), jnp.zeros((), bf16)
            )
        added = contract(left[...], right[...])
        for half in range(2):
            sums[half] += added[:, half * LANES : (half + 1) * LANES]

    for half in range(2):
        columns = slice(half * LANES, (half + 1) * LANES)
        total = []
        for term in range(9):
            pieces = [
                sums[half, pl.ds(part * 9 + term, uppers, stride=TERM_ROWS), :]
                for part in range(PARTS)
            ]
            total.append(pieces[0] + (pieces[1] + pieces[2]))
        solved = solve_points(total[:3], total[3:], damping[:, columns])
        for a in range(3):
            answers[pl.ds((a * 2 + half) * uppers, uppers), :] = solved[a]

    @pl.loop(0, groups)
    def _(group):
        base = group * rows
        ids = received[pl.ds(base + 8, GROUP, stride=SLOT_ROWS), :].astype(i32)
        lane = ids & (LANES - 1)
        chunk = ids // LANES
        got = [None] * 3
        for k in range(2 * uppers):
            h, half = k // 2, k % 2
            for a in range(3):
                row = (a * 2 + half) * uppers + h
                table = jnp.broadcast_to(answers[row : row + 1, :], (GROUP, LANES))
                value = lookup(table, lane)
                got[a] = value if k == 0 else jnp.where(chunk == k, value, got[a])
        for r in range(2):
            image = sum(
                received[pl.ds(base + 3 * r + a, GROUP, stride=SLOT_ROWS), :] * got[a]
                for a in range(3)
            )
            error = received[pl.ds(base + 6 + r, GROUP, stride=SLOT_ROWS), :]
            remain[pl.ds(group * 2 * GROUP + r, GROUP, stride=2), :] = error - image


def camera_kernel(slots, remain, cam_jac, cam_ids, image, pieces, left, right):
    tiles = cam_ids.shape[0]
    cams = right.shape[0]
    copies = image.shape[0] // 18
    row = lax.broadcasted_iota(i32, (18, LANES), 0)
    cam_of_row = lax.broadcasted_iota(i32, (cams, LANES), 0).astype(bf16)
    pieces[...] = jnp.zeros(pieces.shape, f32)

    def step(group, total):
        for s in range(GROUP):
            tile = group * GROUP + s
            columns = slice(s * LANES, (s + 1) * LANES)
            base = slots[tile] * 2
            value = cam_jac[tile] * jnp.where(
                row < 9, remain[pl.ds(base, 1), :], remain[pl.ds(base + 1, 1), :]
            )
            pieces[s * TERM_ROWS : s * TERM_ROWS + 18, :] = value
            block = pieces[s * TERM_ROWS : (s + 1) * TERM_ROWS, :]
            for part, piece in enumerate(split(block)):
                left[part * TERM_ROWS : (part + 1) * TERM_ROWS, columns] = piece.astype(bf16)
            ids = jnp.broadcast_to(cam_ids[pl.ds(tile, 1), :], (cams, LANES)).astype(f32)
            right[:, columns] = jnp.where(
                cam_of_row == ids.astype(bf16), jnp.ones((), bf16), jnp.zeros((), bf16)
            )
        return total + contract(left[...], right[...])

    total = lax.fori_loop(
        0, tiles // GROUP, step, jnp.zeros((PARTS * TERM_ROWS, cams), f32)
    )
    merged = total[0:32] + (total[32:64] + total[64:96])
    for half in range(2):
        pieces[0:32, :] = merged[:, half * LANES : (half + 1) * LANES]
        summed = pieces[0:9, :] + pieces[9:18, :]
        for copy in range(copies):
            image[copy * 18 + half * 9 : copy * 18 + half * 9 + 9, :] = summed


def apply_blocks(precond, vector):
    total = None
    for j in range(9):
        term = precond[9 * j : 9 * j + 9, :] * vector[j : j + 1, :]
        total = term if total is None else total + term
    return total


def scalar_kernel(received, residual, direction, damping, precond, image, first_z, slope, scalars):
    copies = received.shape[0] // 18
    for half in range(2):
        columns = slice(half * LANES, (half + 1) * LANES)
        total = received[half * 9 : half * 9 + 9, :]
        for copy in range(1, copies):
            total = total + received[copy * 18 + half * 9 : copy * 18 + half * 9 + 9, :]
        image[:, columns] = damping[:, columns] * direction[:, columns] + total
    z = apply_blocks(precond, residual)
    y = apply_blocks(precond, image)
    first_z[...] = z
    slope[...] = y
    res = residual[...]
    img = image[...]
    sums = [
        jnp.sum(res * z),
        jnp.sum(direction[...] * img),
        jnp.sum(img * z + res * y),
        jnp.sum(img * y),
    ]
    lane = lax.broadcasted_iota(i32, scalars.shape, 1)
    row = jnp.zeros(scalars.shape, f32)
    for k, value in enumerate(sums):
        row = jnp.where(lane == k, value, row)
    scalars[...] = row


def final_kernel(
    scalars,
    solution_in,
    residual,
    direction,
    image,
    first_z,
    slope,
    new_solution,
    new_residual,
    new_direction,
):
    total = jnp.sum(scalars[...], axis=0, keepdims=True)
    lane = lax.broadcasted_iota(i32, total.shape, 1)
    rz, pq, cross, square = [
        jnp.sum(jnp.where(lane == k, total, 0.0), axis=1, keepdims=True) for k in range(4)
    ]
    alpha = rz / pq
    rz1 = rz + alpha * (alpha * square - cross)
    way = direction[...]
    new_solution[...] = solution_in[...] + alpha * way
    new_residual[...] = residual[...] - alpha * image[...]
    new_direction[...] = first_z[...] - alpha * slope[...] + (rz1 / rz) * way


SMEM = pl.BlockSpec(memory_space=pltpu.SMEM)
VMEM = pl.BlockSpec(memory_space=pltpu.VMEM)
LIMIT = pltpu.CompilerParams(vmem_limit_bytes=32 * 1024 * 1024)


def shape(*dims, dtype=f32):
    return jax.ShapeDtypeStruct(dims, dtype)


def pack(owners, counts, direction, cam_ids, cam_jac, pt_jac, point_ids, owner_count):
    tiles = cam_ids.shape[0]
    return pl.pallas_call(
        pack_kernel,
        out_shape=(
            shape(owner_count * PER_OWNER * SLOT_ROWS, LANES),
            shape(tiles, dtype=i32),
        ),
        in_specs=[SMEM, SMEM] + [VMEM] * 5,
        out_specs=(VMEM, SMEM),
        scratch_shapes=[
            pltpu.SMEM((owner_count,), i32),
            pltpu.VMEM((24, direction.shape[1]), f32),
        ],
        compiler_params=LIMIT,
        name="pack_tiles",
    )(owners, counts, direction, cam_ids, cam_jac, pt_jac, point_ids)


def points(received, damping):
    slots = received.shape[0] // SLOT_ROWS
    uppers = damping.shape[0]
    return pl.pallas_call(
        point_kernel,
        out_shape=shape(slots * 2, LANES),
        in_specs=[VMEM] * 2,
        out_specs=VMEM,
        scratch_shapes=[
            pltpu.VMEM((GROUP * TERM_ROWS, LANES), f32),
            pltpu.VMEM((uppers * TERM_ROWS, GROUP * LANES), bf16),
            pltpu.VMEM((POINT_LOW, GROUP * LANES), bf16),
            pltpu.VMEM((2, uppers * TERM_ROWS, LANES), f32),
            pltpu.VMEM((6 * uppers, LANES), f32),
        ],
        compiler_params=LIMIT,
        name="solve_points",
    )(received, damping)


def cameras(slots, remain, cam_jac, cam_ids, cams, copies):
    return pl.pallas_call(
        camera_kernel,
        out_shape=shape(copies * 18, LANES),
        in_specs=[SMEM] + [VMEM] * 3,
        out_specs=VMEM,
        scratch_shapes=[
            pltpu.VMEM((GROUP * TERM_ROWS, LANES), f32),
            pltpu.VMEM((PARTS * TERM_ROWS, GROUP * LANES), bf16),
            pltpu.VMEM((cams, GROUP * LANES), bf16),
        ],
        compiler_params=LIMIT,
        name="sum_cameras",
    )(slots, remain, cam_jac, cam_ids)


def scalar_sums(received, residual, direction, damping, precond, owner_count):
    vector = shape(*residual.shape)
    return pl.pallas_call(
        scalar_kernel,
        out_shape=(vector, vector, vector, shape(owner_count, LANES)),
        in_specs=[VMEM] * 5,
        out_specs=(VMEM,) * 4,
        compiler_params=LIMIT,
        name="camera_scalars",
    )(received, residual, direction, damping, precond)


def finish(scalars, solution_in, residual, direction, image, first_z, slope):
    vector = shape(*residual.shape)
    return pl.pallas_call(
        final_kernel,
        out_shape=(vector,) * 3,
        in_specs=[VMEM] * 7,
        out_specs=(VMEM,) * 3,
        compiler_params=LIMIT,
        name="update_vectors",
    )(scalars, solution_in, residual, direction, image, first_z, slope)


def exchange(rows, axis, count):
    depth = rows.shape[0] // count
    sent = rows.reshape(count, depth, 1, LANES)
    got = lax.all_to_all(sent, axis, split_axis=0, concat_axis=0, tiled=True)
    return got.reshape(count * depth, LANES)


def body(
    solution,
    residual,
    direction,
    cam_damping,
    precond,
    pt_damping,
    cam_jac,
    pt_jac,
    cam_ids,
    point_ids,
    owners,
    valid_counts,
):
    owner_count = lax.axis_size("cam")
    copies = lax.axis_size("pt")
    payload, slots = pack(
        owners.reshape(-1),
        valid_counts,
        direction,
        cam_ids,
        cam_jac,
        pt_jac,
        point_ids,
        owner_count,
    )
    received = exchange(payload, "cam", owner_count)
    remain = points(received, pt_damping.reshape(-1, POINT_LOW))
    returned = exchange(remain, "cam", owner_count)
    image_rows = cameras(slots, returned, cam_jac, cam_ids, direction.shape[1], copies)
    image_all = exchange(image_rows, "pt", copies)
    image, first_z, slope, scalars = scalar_sums(
        image_all, residual, direction, cam_damping, precond, owner_count
    )
    scalars_all = exchange(scalars, "cam", owner_count)
    return finish(scalars_all, solution, residual, direction, image, first_z, slope)


def solution(mesh):
    return jax.shard_map(
        body,
        mesh=mesh,
        in_specs=(
            P(None, "cam"),
            P(None, "cam"),
            P(None, "cam"),
            P(None, "cam"),
            P(None, "cam"),
            P(("cam", "pt")),
            P(("cam", "pt"), None, None),
            P(("cam", "pt"), None, None),
            P(("cam", "pt"), None),
            P(("cam", "pt"), None),
            P(("cam", "pt"), None),
            P(("cam", "pt")),
        ),
        out_specs=(P(None, "cam"), P(None, "cam"), P(None, "cam")),
        check_vma=False,
    )
```

time: 616 us -> 99.8 us (0.16)
  blocking collectives: 324 us -> 48.6 us
  other arithmetic: 157 us -> 0 us
  local copies, waits for them, and re-layouts: 111 us -> 2.3 us
  Pallas kernels: 0 us -> 17 us
  waiting for transfers between devices: 12.4 us -> 19 us
    psum x3 -> x0, blocking collectives: 285 us -> none  [the longest x1 131 us: body(): product_rz = lax.psum(local_rz, 'cam')]
    scatter-add x2 -> x0, other arithmetic: 147 us -> none  [the longest x1 102 us: body(): jnp.zeros((9, pt_damping.shape[0]), jnp.float32).at[:, recv_ids.reshape(-1)]]
    gather x5 -> x0, local copies, waits for them, and re-layouts: 91.2 us -> none  [the longest x2 60 us: body(): slot_sol = jnp.take(point_sol, recv_ids, axis=1).transpose(1, 0, 2)]
    pallas_call x0 -> x5, Pallas kernels: none -> 17 us  [the longest x1 9.77 us: points(): pl.pallas_call(point_kernel, out_shape=shape(slots * 2, LANES), in_specs=...]
    all_to_all x1 -> x3, blocking collectives: 39.4 us -> 48.6 us  [exchange(): got = lax.all_to_all(sent, axis, split_axis=0, concat_axis=0, tiled=True)]
    reshape x3 -> x1, local copies, waits for them, and re-layouts: 7.3 us -> 0.01 us  [body(): remain = points(received, pt_damping.reshape(-1, POINT_LOW))]
    all_to_all x1, waiting for transfers between devices: 12.4 us -> 19 us  [exchange(): got = lax.all_to_all(sent, axis, split_axis=0, concat_axis=0, tiled=True)]
where the time goes in v1:
time: 99.8 us; the launch traced here: 99.4 us
  blocking collectives  48.6 us (49%)
  waiting for transfers between devices  19 us (19%)
  Pallas kernels  17 us (17%)
  starting transfers between devices  11.6 us (12%)
  local copies, waits for them, and re-layouts  2.3 us (2%)
    all_to_all x3, blocking collectives, exchange(): got = lax.all_to_all(sent, axis, split_axis=0, concat_axis=0, tiled=True)  48.6 us
    all_to_all x1, waiting for transfers between devices, exchange(): got = lax.all_to_all(sent, axis, split_axis=0, concat_axis=0, tiled=True)  19 us
    all_to_all x1, starting transfers between devices, exchange(): got = lax.all_to_all(sent, axis, split_axis=0, concat_axis=0, tiled=True)  11.6 us
    pallas_call x1, Pallas kernels, points(): pl.pallas_call(point_kernel, out_shape=shape(slots * 2, LANES), in_specs=...  9.77 us
    pallas_call x1, Pallas kernels, cameras(): pl.pallas_call(camera_kernel, out_shape=shape(copies * 18, LANES), in_spe...  3.34 us
    pallas_call x1, Pallas kernels, pack(): pl.pallas_call(pack_kernel, out_shape=(shape(owner_count * PER_OWNER * SL...  3.01 us
    unnamed x24, local copies, waits for them, and re-layouts  2.29 us
  transfers between devices with their start and end apart: 1, of which 1 were waited for; matrix products, arithmetic and copies ran while one was open for 0% of the time, Pallas kernels for 0%

profile of v1, /device:TPU:1, one launch (start us, length us, event | category | flops | bytes accessed | tf_op | source)
XLA Modules:
  0.0 99.4 jit_solution(12442100192165928821)
XLA Ops:
  0.6 1.5 %copy.21.cam_jac = f32[64,18,128]{2,1,0:T(8,128)S(1)} copy(f32[64,18,128]{2,0,1:T(8,128)} %param.18) | data formatting | bytes 1179648 | tf_op args[6]
  2.1 0.0 copy-start
  2.1 0.0 copy-start.1
  2.1 0.0 copy-start.4
  2.1 0.1 copy.22.pt_jac
  2.3 0.0 copy-start.7
  2.3 0.0 copy-start.8
  2.3 0.5 copy-done
  2.8 0.1 copy-done.1
  2.9 0.0 copy-done.4
  2.9 0.0 copy-done.7
  2.9 0.0 copy-done.8
  3.0 3.0 %pack_tiles.1 = (f32[1152,128]{1,0:T(8,128)}, s32[64]{0:T(128)S(1)}) custom-call(s32[64]{0:T(128)S(1)} %bitcast.20, s32[64]{0:T(128)S(1)} %copy-done.8, f32[9,256]{1,0:T(8,128)S(1)} %copy-done, s32[64,128]{1,0:T(8,128)S(1)} %copy-done.1, f32[64,18,128]{2,1,0:T(8,128)S(1)} %copy.21.cam_jac, f32[64,6,128]{2,1,0:T(8,128)S(1)} %copy.22.pt_jac, ...), custom_call_target="tpu_custom_call" | custom-call | tf_op jit(solution)/shard_map/pack_tiles/pallas_call | solution.py:292
  6.0 0.0 copy-start.10
  6.0 11.6 %all-to-all-start = ((f32[64,18,1,128]{3,2,1,0:T(1,128)}), f32[64,18,1,128]{3,2,1,0:T(1,128)S(1)}, u32[]{:S(2)}, u32[]{:S(2)}) async-start(f32[64,18,1,128]{3,2,1,0:T(1,128)} %bitcast.1), calls=%async_computation | async-start | bytes 1179648 | tf_op jit(solution)/shard_map/all_to_all | solution.py:372
  17.7 19.0 %all-to-all-done = f32[64,18,1,128]{3,2,1,0:T(1,128)S(1)} async-done(((f32[64,18,1,128]{3,2,1,0:T(1,128)}), f32[64,18,1,128]{3,2,1,0:T(1,128)S(1)}, u32[]{:S(2)}, u32[]{:S(2)}) %all-to-all-start) | async-done | bytes 589856 | tf_op jit(solution)/shard_map/all_to_all | solution.py:372
  36.7 9.8 %solve_points.1 = f32[256,128]{1,0:T(8,128)S(1)} custom-call(f32[1152,128]{1,0:T(8,128)S(1)} %bitcast.13, f32[8,256]{1,0:T(8,128)S(1)} %reshape.39.damping), custom_call_target="tpu_custom_call" | custom-call | tf_op jit(solution)/shard_map/solve_points/pallas_call | solution.py:312
  46.5 16.7 %all_to_all.20 = f32[64,4,1,128]{3,1,2,0:T(4,128)S(1)} all-to-all(f32[64,4,1,128]{3,1,2,0:T(4,128)S(1)} %bitcast.15), channel_id=1, replica_groups=mesh['cam'=64,'pt'=8] {'cam'}, dimensions={0} | all-to-all | bytes 262144 | tf_op jit(solution)/shard_map/all_to_all | solution.py:372
  63.1 3.3 %sum_cameras.1 = f32[144,128]{1,0:T(8,128)S(1)} custom-call(s32[64]{0:T(128)S(1)} %get-tuple-element.9.slots, f32[256,128]{1,0:T(8,128)S(1)} %bitcast.14, f32[64,18,128]{2,1,0:T(8,128)S(1)} %copy.21.cam_jac, s32[64,128]{1,0:T(8,128)S(1)} %copy-done.1), custom_call_target="tpu_custom_call" | custom-call | tf_op jit(solution)/shard_map/sum_cameras/pallas_call | solution.py:330
  66.5 0.0 copy-start.2
  66.5 17.2 %all_to_all.21 = f32[8,18,1,128]{3,2,1,0:T(1,128)S(1)} all-to-all(f32[8,18,1,128]{3,2,1,0:T(1,128)S(1)} %bitcast.16), channel_id=1, replica_groups=mesh['cam'=64,'pt'=8] {'pt'}, dimensions={0} | all-to-all | bytes 147456 | tf_op jit(solution)/shard_map/all_to_all | solution.py:372
  83.7 0.2 camera_scalars.1
  83.9 14.7 %all_to_all.22 = f32[64,1,1,128]{3,2,1,0:T(1,128)S(1)} all-to-all(f32[64,1,1,128]{3,2,1,0:T(1,128)S(1)} %bitcast.19), channel_id=1, replica_groups=mesh['cam'=64,'pt'=8] {'cam'}, dimensions={0} | all-to-all | bytes 65536 | tf_op jit(solution)/shard_map/all_to_all | solution.py:372
  98.6 0.7 update_vectors.1
  (11 shorter events, 0.0 us)
Async XLA Ops:
  0.6 1.5 %copy-start.9 = (f32[64,6,128]{2,0,1:T(8,128)S(1)}, f32[64,6,128]{2,0,1:T(8,128)}, u32[]{:S(2)}) copy-start(f32[64,6,128]{2,0,1:T(8,128)} %param.19) | copy-start | bytes 589828
  2.1 0.7 copy-start
  2.1 0.8 copy-start.1
  2.1 0.8 copy-start.4
  2.3 0.7 copy-start.7
  2.3 0.7 copy-start.8
  6.0 11.7 %copy-start.10 = (f32[2048]{0:T(1024)S(1)}, f32[2048]{0:T(1024)}, u32[]{:S(2)}) copy-start(f32[2048]{0:T(1024)} %param.17) | copy-start | bytes 24580
  6.0 30.7 %all-to-all-start = ((f32[64,18,1,128]{3,2,1,0:T(1,128)}), f32[64,18,1,128]{3,2,1,0:T(1,128)S(1)}, u32[]{:S(2)}, u32[]{:S(2)}) async-start(f32[64,18,1,128]{3,2,1,0:T(1,128)} %bitcast.1), calls=%async_computation | async-start | bytes 1179648 | tf_op jit(solution)/shard_map/all_to_all | solution.py:372
  66.5 17.2 %copy-start.2 = (f32[81,256]{1,0:T(8,128)S(1)}, f32[81,256]{1,0:T(8,128)}, u32[]{:S(2)}) copy-start(f32[81,256]{1,0:T(8,128)} %precond.1) | copy-start | bytes 248836
  66.5 17.2 %copy-start.3 = (f32[9,256]{1,0:T(8,128)S(1)}, f32[9,256]{1,0:T(8,128)}, u32[]{:S(2)}) copy-start(f32[9,256]{1,0:T(8,128)} %residual.3) | copy-start | bytes 27652
  66.5 17.2 %copy-start.5 = (f32[9,256]{1,0:T(8,128)S(1)}, f32[9,256]{1,0:T(8,128)}, u32[]{:S(2)}) copy-start(f32[9,256]{1,0:T(8,128)} %damping.1) | copy-start | bytes 27652
  83.9 14.7 %copy-start.6 = (f32[9,256]{1,0:T(8,128)S(1)}, f32[9,256]{1,0:T(8,128)}, u32[]{:S(2)}) copy-start(f32[9,256]{1,0:T(8,128)} %solution_in.1) | copy-start | bytes 27652

commit v2 on v1

--- a/solution.py
+++ b/solution.py
@@ -14,6 +14,8 @@
 GROUP = 8
 POINT_LOW = 256
 PARTS = 3
+CHUNK = 2
+PLACES = 2
 
 f32 = jnp.float32
 bf16 = jnp.bfloat16
@@ -36,52 +38,66 @@
     return lax.dot_general(left, right, (((1,), (1,)), ((), ())), preferred_element_type=f32)
 
 
+def store_terms(terms, values, group):
+    base = group * GROUP * TERM_ROWS
+    for term, value in enumerate(values):
+        for part, piece in enumerate(split(value)):
+            terms[pl.ds(base + part * 9 + term, GROUP, stride=TERM_ROWS), :] = piece
+
+
+def one_hot(row_index, ids):
+    return jnp.where(row_index == ids, jnp.ones((), bf16), jnp.zeros((), bf16))
+
+
+def spread(value, s, rows):
+    return jnp.broadcast_to(value[s : s + 1, :], (rows, LANES)).astype(bf16)
+
+
 def pack_kernel(
-    owners, counts, direction, cam_ids, cam_jac, pt_jac, point_ids, payload, slots, seen, table
+    owners, counts, direction, cam_ids, cam_jac, pt_jac, point_ids, payload, slots, seen, stage
 ):
-    tiles, width = cam_ids.shape
-    owner_count = seen.shape[0]
+    tiles = cam_ids.shape[0]
     payload[...] = jnp.zeros(payload.shape, f32)
-
-    @pl.loop(0, owner_count)
-    def _(index):
+    for index in range(seen.shape[0]):
         seen[index] = 0
-
-    table[0:9, :] = direction[...]
-    table[9:18, :] = direction[...]
-    table[18:24, :] = jnp.zeros((6, table.shape[1]), f32)
-    tables = [
-        [table[8 * g : 8 * g + 8, LANES * c : LANES * (c + 1)] for c in range(2)] for g in range(3)
-    ]
-    lane = lax.broadcasted_iota(i32, (1, LANES), 1)
-    row8 = lax.broadcasted_iota(i32, (8, LANES), 0)
-
-    @pl.loop(0, tiles, unroll=8)
-    def _(tile):
+    lane = lax.broadcasted_iota(i32, (GROUP, LANES), 1)
+    row = lax.broadcasted_iota(i32, (GROUP, LANES), 0)
+    for group in range(tiles // GROUP):
+        span = slice(group * GROUP, (group + 1) * GROUP)
+        ids = cam_ids[span, :]
+        low = ids & (LANES - 1)
+        upper = ids >= LANES
+        errors = [None, None]
+        for j in range(9):
+            tables = [
+                jnp.broadcast_to(direction[j : j + 1, LANES * c : LANES * (c + 1)], (GROUP, LANES))
+                for c in range(2)
+            ]
+            picked = jnp.where(upper, lookup(tables[1], low), lookup(tables[0], low))
+            for r in range(2):
+                term = cam_jac[9 * r + j, span, :] * picked
+                errors[r] = term if errors[r] is None else errors[r] + term
+        used = jnp.zeros((GROUP, LANES), i32)
+        for s in range(GROUP):
+            used = jnp.where(row == s, counts[group * GROUP + s], used)
+        valid = lane < used
+        values = [pt_jac[a, span, :] for a in range(6)] + errors
+        for r, value in enumerate(values):
+            stage[pl.ds(group * GROUP * SLOT_ROWS + r, GROUP, stride=SLOT_ROWS), :] = jnp.where(
+                valid, value, 0.0
+            )
+        stage[pl.ds(group * GROUP * SLOT_ROWS + 8, GROUP, stride=SLOT_ROWS), :] = point_ids[
+            span, :
+        ].astype(f32)
+    for tile in range(tiles):
         owner = owners[tile]
         rank = seen[owner]
         seen[owner] = rank + 1
         slot = owner * PER_OWNER + rank
         slots[tile] = slot
-        base = slot * SLOT_ROWS
-        ids = jnp.broadcast_to(cam_ids[pl.ds(tile, 1), :], (8, LANES))
-        low = ids & (LANES - 1)
-        upper = ids >= LANES
-        picked = [
-            jnp.where(upper, lookup(tables[g][1], low), lookup(tables[g][0], low)) for g in range(3)
+        payload[pl.ds(slot * SLOT_ROWS, SLOT_ROWS), :] = stage[
+            tile * SLOT_ROWS : (tile + 1) * SLOT_ROWS, :
         ]
-        first = cam_jac[tile, 0:8, :] * picked[0]
-        second = cam_jac[tile, 8:16, :] * picked[1]
-        third = cam_jac[tile, 16:18, :] * picked[2][0:2]
-        valid = lane < counts[tile]
-        err0 = jnp.sum(first + jnp.where(row8 < 1, second, 0.0), axis=0, keepdims=True)
-        err1 = jnp.sum(jnp.where(row8 < 1, 0.0, second), axis=0, keepdims=True) + jnp.sum(
-            third, axis=0, keepdims=True
-        )
-        payload[pl.ds(base, 6), :] = jnp.where(valid, pt_jac[tile], 0.0)
-        payload[pl.ds(base + 6, 1), :] = jnp.where(valid, err0, 0.0)
-        payload[pl.ds(base + 7, 1), :] = jnp.where(valid, err1, 0.0)
-        payload[pl.ds(base + 8, 1), :] = point_ids[pl.ds(tile, 1), :].astype(f32)
 
 
 def solve_points(rhs, normal, damping):
@@ -105,7 +121,7 @@
     )
 
 
-def point_kernel(received, damping, remain, terms, left, right, sums, answers):
+def point_kernel(received, damping, remain, terms, sums, answers):
     slots = remain.shape[0] // 2
     groups = slots // GROUP
     uppers = damping.shape[0]
@@ -114,36 +130,42 @@
     sums[...] = jnp.zeros(sums.shape, f32)
     low_of_row = lax.broadcasted_iota(i32, (POINT_LOW, LANES), 0).astype(bf16)
 
-    @pl.loop(0, groups)
-    def _(group):
-        base = group * rows
-        jac = [received[pl.ds(base + r, GROUP, stride=SLOT_ROWS), :] for r in range(6)]
-        err0 = received[pl.ds(base + 6, GROUP, stride=SLOT_ROWS), :]
-        err1 = received[pl.ds(base + 7, GROUP, stride=SLOT_ROWS), :]
-        ids = received[pl.ds(base + 8, GROUP, stride=SLOT_ROWS), :].astype(i32)
-        upper = (ids // POINT_LOW).astype(f32)
-        lower = (ids & (POINT_LOW - 1)).astype(f32)
-        values = [jac[a] * err0 + jac[3 + a] * err1 for a in range(3)]
-        for a, b in ((0, 0), (0, 1), (0, 2), (1, 1), (1, 2), (2, 2)):
-            values.append(jac[a] * jac[b] + jac[3 + a] * jac[3 + b])
-        for term, value in enumerate(values):
-            for part, piece in enumerate(split(value)):
-                terms[pl.ds(part * 9 + term, GROUP, stride=TERM_ROWS), :] = piece
-        for s in range(GROUP):
-            columns = slice(s * LANES, (s + 1) * LANES)
-            block = terms[s * TERM_ROWS : (s + 1) * TERM_ROWS, :].astype(bf16)
-            upper_row = jnp.broadcast_to(upper[s : s + 1, :], (TERM_ROWS, LANES)).astype(bf16)
-            lower_row = jnp.broadcast_to(lower[s : s + 1, :], (POINT_LOW, LANES)).astype(bf16)
-            for h in range(uppers):
-                left[h * TERM_ROWS : (h + 1) * TERM_ROWS, columns] = jnp.where(
-                    upper_row == jnp.asarray(h, bf16), block, jnp.zeros_like(block)
+    def chunk(start, place):
+        lefts, rights = [], []
+        for k in range(CHUNK):
+            base = (start + k) * rows
+            jac = [received[pl.ds(base + r, GROUP, stride=SLOT_ROWS), :] for r in range(6)]
+            err0 = received[pl.ds(base + 6, GROUP, stride=SLOT_ROWS), :]
+            err1 = received[pl.ds(base + 7, GROUP, stride=SLOT_ROWS), :]
+            ids = received[pl.ds(base + 8, GROUP, stride=SLOT_ROWS), :].astype(i32)
+            upper = (ids // POINT_LOW).astype(f32)
+            lower = (ids & (POINT_LOW - 1)).astype(f32)
+            values = [jac[a] * err0 + jac[3 + a] * err1 for a in range(3)]
+            for a, b in ((0, 0), (0, 1), (0, 2), (1, 1), (1, 2), (2, 2)):
+                values.append(jac[a] * jac[b] + jac[3 + a] * jac[3 + b])
+            store_terms(terms, values, place * CHUNK + k)
+            for s in range(GROUP):
+                at = ((place * CHUNK + k) * GROUP + s) * TERM_ROWS
+                block = terms[at : at + TERM_ROWS, :].astype(bf16)
+                upper_row = spread(upper, s, TERM_ROWS)
+                lefts.append(
+                    jnp.concatenate(
+                        [
+                            jnp.where(upper_row == jnp.asarray(h, bf16), block, jnp.zeros_like(block))
+                            for h in range(uppers)
+                        ],
+                        axis=0,
+                    )
                 )
-            right[:, columns] = jnp.where(
-                low_of_row == lower_row, jnp.ones((), bf16), jnp.zeros((), bf16)
-            )
-        added = contract(left[...], right[...])
-        for half in range(2):
-            sums[half] += added[:, half * LANES : (half + 1) * LANES]
+                rights.append(one_hot(low_of_row, spread(lower, s, POINT_LOW)))
+        return contract(jnp.concatenate(lefts, axis=1), jnp.concatenate(rights, axis=1))
+
+    @pl.loop(0, groups // (CHUNK * PLACES))
+    def _(step):
+        for place in range(PLACES):
+            added = chunk((step * PLACES + place) * CHUNK, place)
+            for half in range(2):
+                sums[half] += added[:, half * LANES : (half + 1) * LANES]
 
     for half in range(2):
         columns = slice(half * LANES, (half + 1) * LANES)
@@ -181,39 +203,34 @@
             remain[pl.ds(group * 2 * GROUP + r, GROUP, stride=2), :] = error - image
 
 
-def camera_kernel(slots, remain, cam_jac, cam_ids, image, pieces, left, right):
+def camera_kernel(slots, remain, cam_jac, cam_ids, image, terms, stage):
     tiles = cam_ids.shape[0]
-    cams = right.shape[0]
+    cams = 2 * LANES
     copies = image.shape[0] // 18
-    row = lax.broadcasted_iota(i32, (18, LANES), 0)
     cam_of_row = lax.broadcasted_iota(i32, (cams, LANES), 0).astype(bf16)
-    pieces[...] = jnp.zeros(pieces.shape, f32)
-
-    def step(group, total):
-        for s in range(GROUP):
-            tile = group * GROUP + s
-            columns = slice(s * LANES, (s + 1) * LANES)
-            base = slots[tile] * 2
-            value = cam_jac[tile] * jnp.where(
-                row < 9, remain[pl.ds(base, 1), :], remain[pl.ds(base + 1, 1), :]
-            )
-            pieces[s * TERM_ROWS : s * TERM_ROWS + 18, :] = value
-            block = pieces[s * TERM_ROWS : (s + 1) * TERM_ROWS, :]
-            for part, piece in enumerate(split(block)):
-                left[part * TERM_ROWS : (part + 1) * TERM_ROWS, columns] = piece.astype(bf16)
-            ids = jnp.broadcast_to(cam_ids[pl.ds(tile, 1), :], (cams, LANES)).astype(f32)
-            right[:, columns] = jnp.where(
-                cam_of_row == ids.astype(bf16), jnp.ones((), bf16), jnp.zeros((), bf16)
-            )
-        return total + contract(left[...], right[...])
-
-    total = lax.fori_loop(
-        0, tiles // GROUP, step, jnp.zeros((PARTS * TERM_ROWS, cams), f32)
-    )
-    merged = total[0:32] + (total[32:64] + total[64:96])
+    terms[...] = jnp.zeros(terms.shape, f32)
+    for tile in range(tiles):
+        stage[2 * tile : 2 * tile + 2, :] = remain[pl.ds(slots[tile] * 2, 2), :]
+    total = None
+    for start in range(0, tiles // GROUP, CHUNK):
+        lefts, rights = [], []
+        for group in range(start, start + CHUNK):
+            span = slice(group * GROUP, (group + 1) * GROUP)
+            rest = [stage[pl.ds(2 * group * GROUP + r, GROUP, stride=2), :] for r in range(2)]
+            values = [
+                cam_jac[j, span, :] * rest[0] + cam_jac[9 + j, span, :] * rest[1] for j in range(9)
+            ]
+            store_terms(terms, values, group)
+            ids = cam_ids[span, :].astype(f32)
+            for s in range(GROUP):
+                at = (group * GROUP + s) * TERM_ROWS
+                lefts.append(terms[at : at + TERM_ROWS, :].astype(bf16))
+                rights.append(one_hot(cam_of_row, spread(ids, s, cams)))
+        added = contract(jnp.concatenate(lefts, axis=1), jnp.concatenate(rights, axis=1))
+        total = added if total is None else total + added
     for half in range(2):
-        pieces[0:32, :] = merged[:, half * LANES : (half + 1) * LANES]
-        summed = pieces[0:9, :] + pieces[9:18, :]
+        terms[0:TERM_ROWS, :] = total[:, half * LANES : (half + 1) * LANES]
+        summed = terms[0:9, :] + (terms[9:18, :] + terms[18:27, :])
         for copy in range(copies):
             image[copy * 18 + half * 9 : copy * 18 + half * 9 + 9, :] = summed
 
@@ -299,7 +316,7 @@
         out_specs=(VMEM, SMEM),
         scratch_shapes=[
             pltpu.SMEM((owner_count,), i32),
-            pltpu.VMEM((24, direction.shape[1]), f32),
+            pltpu.VMEM((tiles * SLOT_ROWS, LANES), f32),
         ],
         compiler_params=LIMIT,
         name="pack_tiles",
@@ -315,9 +332,7 @@
         in_specs=[VMEM] * 2,
         out_specs=VMEM,
         scratch_shapes=[
-            pltpu.VMEM((GROUP * TERM_ROWS, LANES), f32),
-            pltpu.VMEM((uppers * TERM_ROWS, GROUP * LANES), bf16),
-            pltpu.VMEM((POINT_LOW, GROUP * LANES), bf16),
+            pltpu.VMEM((PLACES * CHUNK * GROUP * TERM_ROWS, LANES), f32),
             pltpu.VMEM((2, uppers * TERM_ROWS, LANES), f32),
             pltpu.VMEM((6 * uppers, LANES), f32),
         ],
@@ -326,16 +341,16 @@
     )(received, damping)
 
 
-def cameras(slots, remain, cam_jac, cam_ids, cams, copies):
+def cameras(slots, remain, cam_jac, cam_ids, copies):
+    tiles = cam_ids.shape[0]
     return pl.pallas_call(
         camera_kernel,
         out_shape=shape(copies * 18, LANES),
         in_specs=[SMEM] + [VMEM] * 3,
         out_specs=VMEM,
         scratch_shapes=[
-            pltpu.VMEM((GROUP * TERM_ROWS, LANES), f32),
-            pltpu.VMEM((PARTS * TERM_ROWS, GROUP * LANES), bf16),
-            pltpu.VMEM((cams, GROUP * LANES), bf16),
+            pltpu.VMEM((tiles * TERM_ROWS, LANES), f32),
+            pltpu.VMEM((2 * tiles, LANES), f32),
         ],
         compiler_params=LIMIT,
         name="sum_cameras",
@@ -389,6 +404,8 @@
 ):
     owner_count = lax.axis_size("cam")
     copies = lax.axis_size("pt")
+    cam_jac = cam_jac.transpose(1, 0, 2)
+    pt_jac = pt_jac.transpose(1, 0, 2)
     payload, slots = pack(
         owners.reshape(-1),
         valid_counts,
@@ -402,7 +419,7 @@
     received = exchange(payload, "cam", owner_count)
     remain = points(received, pt_damping.reshape(-1, POINT_LOW))
     returned = exchange(remain, "cam", owner_count)
-    image_rows = cameras(slots, returned, cam_jac, cam_ids, direction.shape[1], copies)
+    image_rows = cameras(slots, returned, cam_jac, cam_ids, copies)
     image_all = exchange(image_rows, "pt", copies)
     image, first_z, slope, scalars = scalar_sums(
         image_all, residual, direction, cam_damping, precond, owner_count

time: 99.8 us -> 96.7 us (0.969)
  Pallas kernels: 17 us -> 11 us
  local copies, waits for them, and re-layouts: 2.3 us -> 4.93 us
    pallas_call x1, Pallas kernels: 9.77 us -> 6.15 us  [points(): pl.pallas_call(point_kernel, out_shape=shape(slots * 2, LANES), in_specs=...]
    unnamed x24 -> x30, local copies, waits for them, and re-layouts: 2.29 us -> 4.93 us
    pallas_call x1, Pallas kernels: 3.01 us -> 1.7 us  [pack(): pl.pallas_call(pack_kernel, out_shape=(shape(owner_count * PER_OWNER * SL...]
    pallas_call x1, Pallas kernels: 3.34 us -> 2.26 us  [cameras(): pl.pallas_call(camera_kernel, out_shape=shape(copies * 18, LANES), in_spe...]
where the time goes in v2:
time: 96.7 us; the launch traced here: 96 us
  blocking collectives  48.6 us (50%)
  waiting for transfers between devices  19 us (20%)
  starting transfers between devices  11.6 us (12%)
  Pallas kernels  11 us (11%)
  local copies, waits for them, and re-layouts  4.93 us (5%)
    all_to_all x3, blocking collectives, exchange(): got = lax.all_to_all(sent, axis, split_axis=0, concat_axis=0, tiled=True)  48.6 us
    all_to_all x1, waiting for transfers between devices, exchange(): got = lax.all_to_all(sent, axis, split_axis=0, concat_axis=0, tiled=True)  19 us
    all_to_all x1, starting transfers between devices, exchange(): got = lax.all_to_all(sent, axis, split_axis=0, concat_axis=0, tiled=True)  11.6 us
    pallas_call x1, Pallas kernels, points(): pl.pallas_call(point_kernel, out_shape=shape(slots * 2, LANES), in_specs=...  6.15 us
    unnamed x30, local copies, waits for them, and re-layouts  4.93 us
    pallas_call x1, Pallas kernels, cameras(): pl.pallas_call(camera_kernel, out_shape=shape(copies * 18, LANES), in_spe...  2.26 us
  transfers between devices with their start and end apart: 1, of which 1 were waited for; matrix products, arithmetic and copies ran while one was open for 0% of the time, Pallas kernels for 0%

profile of v2, /device:TPU:1, one launch (start us, length us, event | category | flops | bytes accessed | tf_op | source)
XLA Modules:
  0.0 96.0 jit_solution(8319282029443633178)
XLA Ops:
  0.7 0.6 copy-done.12
  1.3 0.0 copy-done.13
  1.3 1.1 %copy-done = f32[64,18,128]{2,0,1:T(8,128)S(1)} copy-done((f32[64,18,128]{2,0,1:T(8,128)S(1)}, f32[64,18,128]{2,0,1:T(8,128)}, u32[]{:S(2)}) %copy-start) | copy-done | bytes 589848
  2.4 0.9 copy-done.2
  3.3 0.7 copy-done.3
  4.0 0.8 copy-done.5
  4.8 0.8 copy-done.9
  5.5 1.7 %pack_tiles.1 = (f32[1152,128]{1,0:T(8,128)}, s32[64]{0:T(128)S(1)}) custom-call(s32[64]{0:T(128)S(1)} %bitcast.25, s32[64]{0:T(128)S(1)} %copy-done.13, f32[9,256]{1,0:T(8,128)S(1)} %copy-done.3, s32[64,128]{1,0:T(8,128)S(1)} %copy-done.5, f32[18,64,128]{2,1,0:T(8,128)S(1)} %bitcast.15, f32[6,64,128]{2,1,0:T(8,128)S(1)} %bitcast.22, s32[64,128]{1,0:T(8,128)S(1)} %copy-done.9), custom_call_target="tpu_custom_call" | custom-call | tf_op jit(solution)/shard_map/pack_tiles/pallas_call | solution.py:309
  7.2 0.0 copy-start.14
  7.3 11.6 %all-to-all-start = ((f32[64,18,1,128]{3,2,1,0:T(1,128)}), f32[64,18,1,128]{3,2,1,0:T(1,128)S(1)}, u32[]{:S(2)}, u32[]{:S(2)}) async-start(f32[64,18,1,128]{3,2,1,0:T(1,128)} %bitcast.3), calls=%async_computation | async-start | bytes 1179648 | tf_op jit(solution)/shard_map/all_to_all | solution.py:387
  18.9 0.0 copy-start.1
  18.9 19.0 %all-to-all-done = f32[64,18,1,128]{3,2,1,0:T(1,128)S(1)} async-done(((f32[64,18,1,128]{3,2,1,0:T(1,128)}), f32[64,18,1,128]{3,2,1,0:T(1,128)S(1)}, u32[]{:S(2)}, u32[]{:S(2)}) %all-to-all-start) | async-done | bytes 589856 | tf_op jit(solution)/shard_map/all_to_all | solution.py:387
  37.9 6.1 %solve_points.1 = f32[256,128]{1,0:T(8,128)S(1)} custom-call(f32[1152,128]{1,0:T(8,128)S(1)} %bitcast.17, f32[8,256]{1,0:T(8,128)S(1)} %reshape.39.damping), custom_call_target="tpu_custom_call" | custom-call | tf_op jit(solution)/shard_map/solve_points/pallas_call | solution.py:329
  44.1 0.0 copy-start.6
  44.1 16.7 %all_to_all.20 = f32[64,4,1,128]{3,1,2,0:T(4,128)S(1)} all-to-all(f32[64,4,1,128]{3,1,2,0:T(4,128)S(1)} %bitcast.19), channel_id=1, replica_groups=mesh['cam'=64,'pt'=8] {'cam'}, dimensions={0} | all-to-all | bytes 262144 | tf_op jit(solution)/shard_map/all_to_all | solution.py:387
  60.8 2.3 %sum_cameras.1 = f32[144,128]{1,0:T(8,128)S(1)} custom-call(s32[64]{0:T(128)S(1)} %get-tuple-element.9.slots, f32[256,128]{1,0:T(8,128)S(1)} %bitcast.18, f32[18,64,128]{2,1,0:T(8,128)S(1)} %bitcast.16, s32[64,128]{1,0:T(8,128)S(1)} %copy-done.6), custom_call_target="tpu_custom_call" | custom-call | tf_op jit(solution)/shard_map/sum_cameras/pallas_call | solution.py:346
  63.1 0.0 copy-start.7
  63.1 0.0 copy-start.4
  63.1 0.0 copy-start.8
  63.1 0.0 copy-start.10
  63.1 17.2 %all_to_all.21 = f32[8,18,1,128]{3,2,1,0:T(1,128)S(1)} all-to-all(f32[8,18,1,128]{3,2,1,0:T(1,128)S(1)} %bitcast.21), channel_id=1, replica_groups=mesh['cam'=64,'pt'=8] {'pt'}, dimensions={0} | all-to-all | bytes 147456 | tf_op jit(solution)/shard_map/all_to_all | solution.py:387
  80.4 0.2 camera_scalars.1
  80.6 14.7 %all_to_all.22 = f32[64,1,1,128]{3,2,1,0:T(1,128)S(1)} all-to-all(f32[64,1,1,128]{3,2,1,0:T(1,128)S(1)} %bitcast.24), channel_id=1, replica_groups=mesh['cam'=64,'pt'=8] {'cam'}, dimensions={0} | all-to-all | bytes 65536 | tf_op jit(solution)/shard_map/all_to_all | solution.py:387
  95.3 0.7 update_vectors.1
  (17 shorter events, 0.0 us)
Async XLA Ops:
  0.6 0.7 copy-start.12
  0.6 0.7 copy-start.13
  1.3 1.1 %copy-start = (f32[64,18,128]{2,0,1:T(8,128)S(1)}, f32[64,18,128]{2,0,1:T(8,128)}, u32[]{:S(2)}) copy-start(f32[64,18,128]{2,0,1:T(8,128)} %param.18) | copy-start | bytes 1769476
  2.4 0.9 copy-start.2
  3.3 0.7 copy-start.3
  4.0 0.8 copy-start.5
  4.8 0.8 copy-start.9
  7.2 11.7 %copy-start.14 = (f32[2048]{0:T(1024)S(1)}, f32[2048]{0:T(1024)}, u32[]{:S(2)}) copy-start(f32[2048]{0:T(1024)} %param.17) | copy-start | bytes 24580
  7.3 30.7 %all-to-all-start = ((f32[64,18,1,128]{3,2,1,0:T(1,128)}), f32[64,18,1,128]{3,2,1,0:T(1,128)S(1)}, u32[]{:S(2)}, u32[]{:S(2)}) async-start(f32[64,18,1,128]{3,2,1,0:T(1,128)} %bitcast.3), calls=%async_computation | async-start | bytes 1179648 | tf_op jit(solution)/shard_map/all_to_all | solution.py:387
  18.9 41.9 %copy-start.1 = (f32[64,18,128]{2,0,1:T(8,128)S(1)}, f32[64,18,128]{2,0,1:T(8,128)}, u32[]{:S(2)}) copy-start(f32[64,18,128]{2,0,1:T(8,128)} %param.18) | copy-start | bytes 1769476
  44.1 16.7 %copy-start.6 = (s32[64,128]{1,0:T(8,128)S(1)}, s32[64,128]{1,0:T(8,128)}, u32[]{:S(2)}) copy-start(s32[64,128]{1,0:T(8,128)} %cam_ids.3) | copy-start | bytes 98308
  63.1 17.3 %copy-start.7 = (f32[81,256]{1,0:T(8,128)S(1)}, f32[81,256]{1,0:T(8,128)}, u32[]{:S(2)}) copy-start(f32[81,256]{1,0:T(8,128)} %precond.1) | copy-start | bytes 248836
  63.1 17.3 %copy-start.4 = (f32[9,256]{1,0:T(8,128)S(1)}, f32[9,256]{1,0:T(8,128)}, u32[]{:S(2)}) copy-start(f32[9,256]{1,0:T(8,128)} %direction.5) | copy-start | bytes 27652
  63.1 17.3 %copy-start.8 = (f32[9,256]{1,0:T(8,128)S(1)}, f32[9,256]{1,0:T(8,128)}, u32[]{:S(2)}) copy-start(f32[9,256]{1,0:T(8,128)} %residual.3) | copy-start | bytes 27652
  63.1 17.2 %copy-start.10 = (f32[9,256]{1,0:T(8,128)S(1)}, f32[9,256]{1,0:T(8,128)}, u32[]{:S(2)}) copy-start(f32[9,256]{1,0:T(8,128)} %damping.1) | copy-start | bytes 27652
  80.6 14.7 %copy-start.11 = (f32[9,256]{1,0:T(8,128)S(1)}, f32[9,256]{1,0:T(8,128)}, u32[]{:S(2)}) copy-start(f32[9,256]{1,0:T(8,128)} %solution_in.1) | copy-start | bytes 27652

commit v3 on v2

--- a/solution.py
+++ b/solution.py
@@ -15,7 +15,9 @@
 POINT_LOW = 256
 PARTS = 3
 CHUNK = 2
-PLACES = 2
+PLACES = 4
+WIDE = 2
+CAM_CHUNK = 4
 
 f32 = jnp.float32
 bf16 = jnp.bfloat16
@@ -53,13 +55,21 @@
     return jnp.broadcast_to(value[s : s + 1, :], (rows, LANES)).astype(bf16)
 
 
-def pack_kernel(
-    owners, counts, direction, cam_ids, cam_jac, pt_jac, point_ids, payload, slots, seen, stage
-):
+def pack_kernel(*refs):
+    sources, (payload, places, seen, stage), held, sem = refs[:7], refs[7:11], refs[11:18], refs[18]
+    copies = [
+        pltpu.make_async_copy(source, target, sem.at[k])
+        for k, (source, target) in enumerate(zip(sources, held))
+    ]
+    for copy in copies:
+        copy.start()
+    payload[...] = jnp.zeros(payload.shape, f32)
+    owners, counts, direction, cam_ids, cam_jac, pt_jac, point_ids = held
     tiles = cam_ids.shape[0]
-    payload[...] = jnp.zeros(payload.shape, f32)
     for index in range(seen.shape[0]):
         seen[index] = 0
+    for copy in copies:
+        copy.wait()
     lane = lax.broadcasted_iota(i32, (GROUP, LANES), 1)
     row = lax.broadcasted_iota(i32, (GROUP, LANES), 0)
     for group in range(tiles // GROUP):
@@ -89,12 +99,13 @@
         stage[pl.ds(group * GROUP * SLOT_ROWS + 8, GROUP, stride=SLOT_ROWS), :] = point_ids[
             span, :
         ].astype(f32)
+    slot_lane = lax.broadcasted_iota(i32, (1, places.shape[1]), 1)
     for tile in range(tiles):
         owner = owners[tile]
         rank = seen[owner]
         seen[owner] = rank + 1
         slot = owner * PER_OWNER + rank
-        slots[tile] = slot
+        places[tile : tile + 1, :] = jnp.where(slot_lane == slot, 1.0, 0.0)
         payload[pl.ds(slot * SLOT_ROWS, SLOT_ROWS), :] = stage[
             tile * SLOT_ROWS : (tile + 1) * SLOT_ROWS, :
         ]
@@ -180,43 +191,54 @@
         for a in range(3):
             answers[pl.ds((a * 2 + half) * uppers, uppers), :] = solved[a]
 
-    @pl.loop(0, groups)
-    def _(group):
-        base = group * rows
-        ids = received[pl.ds(base + 8, GROUP, stride=SLOT_ROWS), :].astype(i32)
-        lane = ids & (LANES - 1)
-        chunk = ids // LANES
-        got = [None] * 3
+    @pl.loop(0, groups // WIDE)
+    def _(step):
+        bases = [(step * WIDE + w) * rows for w in range(WIDE)]
+        ids = [
+            received[pl.ds(base + 8, GROUP, stride=SLOT_ROWS), :].astype(i32) for base in bases
+        ]
+        lanes = [value & (LANES - 1) for value in ids]
+        chunks = [value // LANES for value in ids]
+        got = [[None] * 3 for _ in range(WIDE)]
         for k in range(2 * uppers):
             h, half = k // 2, k % 2
             for a in range(3):
                 row = (a * 2 + half) * uppers + h
                 table = jnp.broadcast_to(answers[row : row + 1, :], (GROUP, LANES))
-                value = lookup(table, lane)
-                got[a] = value if k == 0 else jnp.where(chunk == k, value, got[a])
-        for r in range(2):
-            image = sum(
-                received[pl.ds(base + 3 * r + a, GROUP, stride=SLOT_ROWS), :] * got[a]
-                for a in range(3)
-            )
-            error = received[pl.ds(base + 6 + r, GROUP, stride=SLOT_ROWS), :]
-            remain[pl.ds(group * 2 * GROUP + r, GROUP, stride=2), :] = error - image
-
-
-def camera_kernel(slots, remain, cam_jac, cam_ids, image, terms, stage):
+                for w in range(WIDE):
+                    value = lookup(table, lanes[w])
+                    got[w][a] = value if k == 0 else jnp.where(chunks[w] == k, value, got[w][a])
+        for w, base in enumerate(bases):
+            for r in range(2):
+                image = sum(
+                    received[pl.ds(base + 3 * r + a, GROUP, stride=SLOT_ROWS), :] * got[w][a]
+                    for a in range(3)
+                )
+                error = received[pl.ds(base + 6 + r, GROUP, stride=SLOT_ROWS), :]
+                remain[pl.ds((step * WIDE + w) * 2 * GROUP + r, GROUP, stride=2), :] = error - image
+
+
+def camera_kernel(places, remain, cam_jac, cam_ids, image, terms, stage):
     tiles = cam_ids.shape[0]
     cams = 2 * LANES
     copies = image.shape[0] // 18
     cam_of_row = lax.broadcasted_iota(i32, (cams, LANES), 0).astype(bf16)
     terms[...] = jnp.zeros(terms.shape, f32)
-    for tile in range(tiles):
-        stage[2 * tile : 2 * tile + 2, :] = remain[pl.ds(slots[tile] * 2, 2), :]
+    chosen = places[...].astype(bf16)
+    for r in range(2):
+        high, middle, low = [
+            lax.dot_general(
+                chosen, piece.astype(bf16), (((1,), (0,)), ((), ())), preferred_element_type=f32
+            )
+            for piece in split(remain[pl.ds(r, places.shape[1], stride=2), :])
+        ]
+        stage[r] = high + (middle + low)
     total = None
-    for start in range(0, tiles // GROUP, CHUNK):
+    for start in range(0, tiles // GROUP, CAM_CHUNK):
         lefts, rights = [], []
-        for group in range(start, start + CHUNK):
+        for group in range(start, start + CAM_CHUNK):
             span = slice(group * GROUP, (group + 1) * GROUP)
-            rest = [stage[pl.ds(2 * group * GROUP + r, GROUP, stride=2), :] for r in range(2)]
+            rest = [stage[r, span, :] for r in range(2)]
             values = [
                 cam_jac[j, span, :] * rest[0] + cam_jac[9 + j, span, :] * rest[1] for j in range(9)
             ]
@@ -306,21 +328,25 @@
 
 def pack(owners, counts, direction, cam_ids, cam_jac, pt_jac, point_ids, owner_count):
     tiles = cam_ids.shape[0]
+    inputs = (owners, counts, direction, cam_ids, cam_jac, pt_jac, point_ids)
+    spaces = [pltpu.SMEM] * 2 + [pltpu.VMEM] * 5
     return pl.pallas_call(
         pack_kernel,
         out_shape=(
             shape(owner_count * PER_OWNER * SLOT_ROWS, LANES),
-            shape(tiles, dtype=i32),
+            shape(tiles, owner_count * PER_OWNER),
         ),
-        in_specs=[SMEM, SMEM] + [VMEM] * 5,
-        out_specs=(VMEM, SMEM),
+        in_specs=[pl.BlockSpec(memory_space=pltpu.HBM)] * 7,
+        out_specs=(VMEM, VMEM),
         scratch_shapes=[
             pltpu.SMEM((owner_count,), i32),
             pltpu.VMEM((tiles * SLOT_ROWS, LANES), f32),
-        ],
-        compiler_params=LIMIT,
+        ]
+        + [space(value.shape, value.dtype) for space, value in zip(spaces, inputs)]
+        + [pltpu.SemaphoreType.DMA((7,))],
+        compiler_params=pltpu.CompilerParams(vmem_limit_bytes=60 * 1024 * 1024),
         name="pack_tiles",
-    )(owners, counts, direction, cam_ids, cam_jac, pt_jac, point_ids)
+    )(*inputs)
 
 
 def points(received, damping):
@@ -341,20 +367,20 @@
     )(received, damping)
 
 
-def cameras(slots, remain, cam_jac, cam_ids, copies):
+def cameras(places, remain, cam_jac, cam_ids, copies):
     tiles = cam_ids.shape[0]
     return pl.pallas_call(
         camera_kernel,
         out_shape=shape(copies * 18, LANES),
-        in_specs=[SMEM] + [VMEM] * 3,
+        in_specs=[VMEM] * 4,
         out_specs=VMEM,
         scratch_shapes=[
             pltpu.VMEM((tiles * TERM_ROWS, LANES), f32),
-            pltpu.VMEM((2 * tiles, LANES), f32),
+            pltpu.VMEM((2, tiles, LANES), f32),
         ],
         compiler_params=LIMIT,
         name="sum_cameras",
-    )(slots, remain, cam_jac, cam_ids)
+    )(places, remain, cam_jac, cam_ids)
 
 
 def scalar_sums(received, residual, direction, damping, precond, owner_count):
@@ -406,7 +432,7 @@
     copies = lax.axis_size("pt")
     cam_jac = cam_jac.transpose(1, 0, 2)
     pt_jac = pt_jac.transpose(1, 0, 2)
-    payload, slots = pack(
+    payload, places = pack(
         owners.reshape(-1),
         valid_counts,
         direction,
@@ -419,7 +445,7 @@
     received = exchange(payload, "cam", owner_count)
     remain = points(received, pt_damping.reshape(-1, POINT_LOW))
     returned = exchange(remain, "cam", owner_count)
-    image_rows = cameras(slots, returned, cam_jac, cam_ids, copies)
+    image_rows = cameras(places, returned, cam_jac, cam_ids, copies)
     image_all = exchange(image_rows, "pt", copies)
     image, first_z, slope, scalars = scalar_sums(
         image_all, residual, direction, cam_damping, precond, owner_count

time: 96.7 us -> 91.2 us (0.943)
  local copies, waits for them, and re-layouts: 4.93 us -> 0.06 us
    unnamed x30 -> x18, local copies, waits for them, and re-layouts: 4.93 us -> 0.05 us
where the time goes in v3:
time: 91.2 us; the launch traced here: 90.7 us
  blocking collectives  48.6 us (53%)
  waiting for transfers between devices  19 us (21%)
  starting transfers between devices  11.6 us (13%)
  Pallas kernels  10.7 us (12%)
    all_to_all x3, blocking collectives, exchange(): got = lax.all_to_all(sent, axis, split_axis=0, concat_axis=0, tiled=True)  48.6 us
    all_to_all x1, waiting for transfers between devices, exchange(): got = lax.all_to_all(sent, axis, split_axis=0, concat_axis=0, tiled=True)  19 us
    all_to_all x1, starting transfers between devices, exchange(): got = lax.all_to_all(sent, axis, split_axis=0, concat_axis=0, tiled=True)  11.6 us
    pallas_call x1, Pallas kernels, points(): pl.pallas_call(point_kernel, out_shape=shape(slots * 2, LANES), in_specs=...  5.27 us
    pallas_call x1, Pallas kernels, pack(): pl.pallas_call(pack_kernel, out_shape=(shape(owner_count * PER_OWNER * SL...  2.36 us
    pallas_call x1, Pallas kernels, cameras(): pl.pallas_call(camera_kernel, out_shape=shape(copies * 18, LANES), in_spe...  2.13 us
  transfers between devices with their start and end apart: 1, of which 1 were waited for; matrix products, arithmetic and copies ran while one was open for 0% of the time, Pallas kernels for 0%

profile of v3, /device:TPU:1, one launch (start us, length us, event | category | flops | bytes accessed | tf_op | source)
XLA Modules:
  0.0 90.7 jit_solution(6137233020583986546)
XLA Ops:
  0.6 2.4 %pack_tiles.1 = (f32[1152,128]{1,0:T(8,128)}, f32[64,128]{1,0:T(8,128)}) custom-call(s32[64]{0:T(128)} %bitcast.26, s32[64]{0:T(128)} %refs_1_.1, f32[9,256]{1,0:T(8,128)} %direction.3, s32[64,128]{1,0:T(8,128)} %cam_ids.1, f32[18,64,128]{2,1,0:T(8,128)} %bitcast.15, f32[6,64,128]{2,1,0:T(8,128)} %bitcast.25, s32[64,128]{1,0:T(8,128)} %refs_6_.1), custom_call_target="tpu_custom_call" | custom-call | tf_op jit(solution)/shard_map/pack_tiles/pallas_call | solution.py:333
  3.0 0.0 copy-start.8
  3.0 11.6 %all-to-all-start = ((f32[64,18,1,128]{3,2,1,0:T(1,128)}), f32[64,18,1,128]{3,2,1,0:T(1,128)S(1)}, u32[]{:S(2)}, u32[]{:S(2)}) async-start(f32[64,18,1,128]{3,2,1,0:T(1,128)} %bitcast.24), calls=%async_computation | async-start | bytes 1179648 | tf_op jit(solution)/shard_map/all_to_all | solution.py:413
  14.7 0.0 copy-done.8
  14.7 0.0 copy-start
  14.7 19.0 %all-to-all-done = f32[64,18,1,128]{3,2,1,0:T(1,128)S(1)} async-done(((f32[64,18,1,128]{3,2,1,0:T(1,128)}), f32[64,18,1,128]{3,2,1,0:T(1,128)S(1)}, u32[]{:S(2)}, u32[]{:S(2)}) %all-to-all-start) | async-done | bytes 589856 | tf_op jit(solution)/shard_map/all_to_all | solution.py:413
  33.7 5.3 %solve_points.1 = f32[256,128]{1,0:T(8,128)S(1)} custom-call(f32[1152,128]{1,0:T(8,128)S(1)} %bitcast.17, f32[8,256]{1,0:T(8,128)S(1)} %reshape.39.damping), custom_call_target="tpu_custom_call" | custom-call | tf_op jit(solution)/shard_map/solve_points/pallas_call | solution.py:355
  39.0 0.0 copy-start.2
  39.0 0.0 copy-start.5
  39.0 16.7 %all_to_all.20 = f32[64,4,1,128]{3,1,2,0:T(4,128)S(1)} all-to-all(f32[64,4,1,128]{3,1,2,0:T(4,128)S(1)} %bitcast.19), channel_id=1, replica_groups=mesh['cam'=64,'pt'=8] {'cam'}, dimensions={0} | all-to-all | bytes 262144 | tf_op jit(solution)/shard_map/all_to_all | solution.py:413
  55.7 0.0 copy-done.2
  55.7 2.1 %sum_cameras.1 = f32[144,128]{1,0:T(8,128)S(1)} custom-call(f32[64,128]{1,0:T(8,128)S(1)} %copy-done.5, f32[256,128]{1,0:T(8,128)S(1)} %bitcast.18, f32[18,64,128]{2,1,0:T(8,128)S(1)} %bitcast.16, s32[64,128]{1,0:T(8,128)S(1)} %copy-done.2), custom_call_target="tpu_custom_call" | custom-call | tf_op jit(solution)/shard_map/sum_cameras/pallas_call | solution.py:372
  57.8 0.0 copy-start.3
  57.9 0.0 copy-start.1
  57.9 0.0 copy-start.4
  57.9 0.0 copy-start.6
  57.9 17.2 %all_to_all.21 = f32[8,18,1,128]{3,2,1,0:T(1,128)S(1)} all-to-all(f32[8,18,1,128]{3,2,1,0:T(1,128)S(1)} %bitcast.21), channel_id=1, replica_groups=mesh['cam'=64,'pt'=8] {'pt'}, dimensions={0} | all-to-all | bytes 147456 | tf_op jit(solution)/shard_map/all_to_all | solution.py:413
  75.1 0.0 copy-done.3
  75.1 0.0 copy-done.4
  75.1 0.2 camera_scalars.1
  75.3 0.0 copy-start.7
  75.3 14.7 %all_to_all.22 = f32[64,1,1,128]{3,2,1,0:T(1,128)S(1)} all-to-all(f32[64,1,1,128]{3,2,1,0:T(1,128)S(1)} %bitcast.23), channel_id=1, replica_groups=mesh['cam'=64,'pt'=8] {'cam'}, dimensions={0} | all-to-all | bytes 65536 | tf_op jit(solution)/shard_map/all_to_all | solution.py:413
  90.0 0.0 copy-done.7
  90.0 0.7 update_vectors.1
  (5 shorter events, 0.0 us)
Async XLA Ops:
  3.0 11.7 %copy-start.8 = (f32[2048]{0:T(1024)S(1)}, f32[2048]{0:T(1024)}, u32[]{:S(2)}) copy-start(f32[2048]{0:T(1024)} %param.17) | copy-start | bytes 24580
  3.0 30.7 %all-to-all-start = ((f32[64,18,1,128]{3,2,1,0:T(1,128)}), f32[64,18,1,128]{3,2,1,0:T(1,128)S(1)}, u32[]{:S(2)}, u32[]{:S(2)}) async-start(f32[64,18,1,128]{3,2,1,0:T(1,128)} %bitcast.24), calls=%async_computation | async-start | bytes 1179648 | tf_op jit(solution)/shard_map/all_to_all | solution.py:413
  14.7 41.0 %copy-start = (f32[64,18,128]{2,0,1:T(8,128)S(1)}, f32[64,18,128]{2,0,1:T(8,128)}, u32[]{:S(2)}) copy-start(f32[64,18,128]{2,0,1:T(8,128)} %param.18) | copy-start | bytes 1769476
  39.0 16.7 %copy-start.2 = (s32[64,128]{1,0:T(8,128)S(1)}, s32[64,128]{1,0:T(8,128)}, u32[]{:S(2)}) copy-start(s32[64,128]{1,0:T(8,128)} %cam_ids.1) | copy-start | bytes 98308
  39.0 16.7 %copy-start.5 = (f32[64,128]{1,0:T(8,128)S(1)}, f32[64,128]{1,0:T(8,128)}, u32[]{:S(2)}) copy-start(f32[64,128]{1,0:T(8,128)} %get-tuple-element.9.places) | copy-start | bytes 98308
  57.8 17.2 %copy-start.3 = (f32[81,256]{1,0:T(8,128)S(1)}, f32[81,256]{1,0:T(8,128)}, u32[]{:S(2)}) copy-start(f32[81,256]{1,0:T(8,128)} %precond.1) | copy-start | bytes 248836
  57.9 17.2 %copy-start.1 = (f32[9,256]{1,0:T(8,128)S(1)}, f32[9,256]{1,0:T(8,128)}, u32[]{:S(2)}) copy-start(f32[9,256]{1,0:T(8,128)} %direction.3) | copy-start | bytes 27652
  57.9 17.2 %copy-start.4 = (f32[9,256]{1,0:T(8,128)S(1)}, f32[9,256]{1,0:T(8,128)}, u32[]{:S(2)}) copy-start(f32[9,256]{1,0:T(8,128)} %residual.3) | copy-start | bytes 27652
  57.9 17.2 %copy-start.6 = (f32[9,256]{1,0:T(8,128)S(1)}, f32[9,256]{1,0:T(8,128)}, u32[]{:S(2)}) copy-start(f32[9,256]{1,0:T(8,128)} %damping.1) | copy-start | bytes 27652
  75.3 14.7 %copy-start.7 = (f32[9,256]{1,0:T(8,128)S(1)}, f32[9,256]{1,0:T(8,128)}, u32[]{:S(2)}) copy-start(f32[9,256]{1,0:T(8,128)} %solution_in.1) | copy-start | bytes 27652

commit v4 on v3

--- a/solution.py
+++ b/solution.py
@@ -9,7 +9,7 @@
 
 LANES = 128
 PER_OWNER = 2
-SLOT_ROWS = 9
+SLOT_ROWS = 8
 TERM_ROWS = 32
 GROUP = 8
 POINT_LOW = 256
@@ -55,8 +55,24 @@
     return jnp.broadcast_to(value[s : s + 1, :], (rows, LANES)).astype(bf16)
 
 
+def turn_of(first, second):
+    largest = jnp.maximum(jnp.abs(first), jnp.abs(second))
+    zero = largest == 0.0
+    scale = jnp.where(zero, 1.0, largest)
+    along = jnp.where(zero, 1.0, first / scale)
+    across = second / scale
+    root = jnp.sqrt(along * along + across * across)
+    return along / root, across / root, largest * root
+
+
+def turn(cosine, sine, first, second):
+    return cosine * first + sine * second, cosine * second - sine * first
+
+
 def pack_kernel(*refs):
-    sources, (payload, places, seen, stage), held, sem = refs[:7], refs[7:11], refs[11:18], refs[18]
+    sources, outputs, held, sem = refs[:7], refs[7:10], refs[12:19], refs[19]
+    payload, places, turns = outputs
+    seen, stage = refs[10:12]
     copies = [
         pltpu.make_async_copy(source, target, sem.at[k])
         for k, (source, target) in enumerate(zip(sources, held))
@@ -91,14 +107,19 @@
         for s in range(GROUP):
             used = jnp.where(row == s, counts[group * GROUP + s], used)
         valid = lane < used
-        values = [pt_jac[a, span, :] for a in range(6)] + errors
+        jac = [jnp.where(valid, pt_jac[a, span, :], 0.0) for a in range(6)]
+        errors = [jnp.where(valid, value, 0.0) for value in errors]
+        cosine, sine, length = turn_of(jac[0], jac[3])
+        turns[0, span, :] = cosine
+        turns[1, span, :] = sine
+        upper_row, lower_row = zip(
+            *[turn(cosine, sine, jac[a], jac[3 + a]) for a in (1, 2)],
+            turn(cosine, sine, *errors),
+        )
+        values = [length, upper_row[0], upper_row[1], lower_row[0], lower_row[1]]
+        values += [upper_row[2], lower_row[2], point_ids[span, :].astype(f32)]
         for r, value in enumerate(values):
-            stage[pl.ds(group * GROUP * SLOT_ROWS + r, GROUP, stride=SLOT_ROWS), :] = jnp.where(
-                valid, value, 0.0
-            )
-        stage[pl.ds(group * GROUP * SLOT_ROWS + 8, GROUP, stride=SLOT_ROWS), :] = point_ids[
-            span, :
-        ].astype(f32)
+            stage[pl.ds(group * GROUP * SLOT_ROWS + r, GROUP, stride=SLOT_ROWS), :] = value
     slot_lane = lax.broadcasted_iota(i32, (1, places.shape[1]), 1)
     for tile in range(tiles):
         owner = owners[tile]
@@ -145,15 +166,18 @@
         lefts, rights = [], []
         for k in range(CHUNK):
             base = (start + k) * rows
-            jac = [received[pl.ds(base + r, GROUP, stride=SLOT_ROWS), :] for r in range(6)]
-            err0 = received[pl.ds(base + 6, GROUP, stride=SLOT_ROWS), :]
-            err1 = received[pl.ds(base + 7, GROUP, stride=SLOT_ROWS), :]
-            ids = received[pl.ds(base + 8, GROUP, stride=SLOT_ROWS), :].astype(i32)
+            first = [received[pl.ds(base + r, GROUP, stride=SLOT_ROWS), :] for r in range(3)]
+            second = [received[pl.ds(base + 3 + r, GROUP, stride=SLOT_ROWS), :] for r in range(2)]
+            err0 = received[pl.ds(base + 5, GROUP, stride=SLOT_ROWS), :]
+            err1 = received[pl.ds(base + 6, GROUP, stride=SLOT_ROWS), :]
+            ids = received[pl.ds(base + 7, GROUP, stride=SLOT_ROWS), :].astype(i32)
             upper = (ids // POINT_LOW).astype(f32)
             lower = (ids & (POINT_LOW - 1)).astype(f32)
-            values = [jac[a] * err0 + jac[3 + a] * err1 for a in range(3)]
-            for a, b in ((0, 0), (0, 1), (0, 2), (1, 1), (1, 2), (2, 2)):
-                values.append(jac[a] * jac[b] + jac[3 + a] * jac[3 + b])
+            values = [first[0] * err0]
+            values += [first[a] * err0 + second[a - 1] * err1 for a in (1, 2)]
+            values += [first[0] * first[a] for a in range(3)]
+            for a, b in ((1, 1), (1, 2), (2, 2)):
+                values.append(first[a] * first[b] + second[a - 1] * second[b - 1])
             store_terms(terms, values, place * CHUNK + k)
             for s in range(GROUP):
                 at = ((place * CHUNK + k) * GROUP + s) * TERM_ROWS
@@ -195,7 +219,7 @@
     def _(step):
         bases = [(step * WIDE + w) * rows for w in range(WIDE)]
         ids = [
-            received[pl.ds(base + 8, GROUP, stride=SLOT_ROWS), :].astype(i32) for base in bases
+            received[pl.ds(base + 7, GROUP, stride=SLOT_ROWS), :].astype(i32) for base in bases
         ]
         lanes = [value & (LANES - 1) for value in ids]
         chunks = [value // LANES for value in ids]
@@ -209,16 +233,19 @@
                     value = lookup(table, lanes[w])
                     got[w][a] = value if k == 0 else jnp.where(chunks[w] == k, value, got[w][a])
         for w, base in enumerate(bases):
+            rows_of = [received[pl.ds(base + r, GROUP, stride=SLOT_ROWS), :] for r in range(7)]
+            y = got[w]
+            images = [
+                rows_of[0] * y[0] + (rows_of[1] * y[1] + rows_of[2] * y[2]),
+                rows_of[3] * y[1] + rows_of[4] * y[2],
+            ]
             for r in range(2):
-                image = sum(
-                    received[pl.ds(base + 3 * r + a, GROUP, stride=SLOT_ROWS), :] * got[w][a]
-                    for a in range(3)
+                remain[pl.ds((step * WIDE + w) * 2 * GROUP + r, GROUP, stride=2), :] = (
+                    rows_of[5 + r] - images[r]
                 )
-                error = received[pl.ds(base + 6 + r, GROUP, stride=SLOT_ROWS), :]
-                remain[pl.ds((step * WIDE + w) * 2 * GROUP + r, GROUP, stride=2), :] = error - image
-
-
-def camera_kernel(places, remain, cam_jac, cam_ids, image, terms, stage):
+
+
+def camera_kernel(places, turns, remain, cam_jac, cam_ids, image, terms, stage):
     tiles = cam_ids.shape[0]
     cams = 2 * LANES
     copies = image.shape[0] // 18
@@ -238,7 +265,8 @@
         lefts, rights = [], []
         for group in range(start, start + CAM_CHUNK):
             span = slice(group * GROUP, (group + 1) * GROUP)
-            rest = [stage[r, span, :] for r in range(2)]
+            cosine, sine = turns[0, span, :], turns[1, span, :]
+            rest = turn(cosine, -sine, stage[0, span, :], stage[1, span, :])
             values = [
                 cam_jac[j, span, :] * rest[0] + cam_jac[9 + j, span, :] * rest[1] for j in range(9)
             ]
@@ -333,11 +361,12 @@
     return pl.pallas_call(
         pack_kernel,
         out_shape=(
-            shape(owner_count * PER_OWNER * SLOT_ROWS, LANES),
-            shape(tiles, owner_count * PER_OWNER),
+            pltpu.VMEM((owner_count * PER_OWNER * SLOT_ROWS, LANES), f32),
+            pltpu.VMEM((tiles, owner_count * PER_OWNER), f32),
+            pltpu.VMEM((2, tiles, LANES), f32),
         ),
         in_specs=[pl.BlockSpec(memory_space=pltpu.HBM)] * 7,
-        out_specs=(VMEM, VMEM),
+        out_specs=(VMEM,) * 3,
         scratch_shapes=[
             pltpu.SMEM((owner_count,), i32),
             pltpu.VMEM((tiles * SLOT_ROWS, LANES), f32),
@@ -367,12 +396,12 @@
     )(received, damping)
 
 
-def cameras(places, remain, cam_jac, cam_ids, copies):
+def cameras(places, turns, remain, cam_jac, cam_ids, copies):
     tiles = cam_ids.shape[0]
     return pl.pallas_call(
         camera_kernel,
         out_shape=shape(copies * 18, LANES),
-        in_specs=[VMEM] * 4,
+        in_specs=[VMEM] * 5,
         out_specs=VMEM,
         scratch_shapes=[
             pltpu.VMEM((tiles * TERM_ROWS, LANES), f32),
@@ -380,7 +409,7 @@
         ],
         compiler_params=LIMIT,
         name="sum_cameras",
-    )(places, remain, cam_jac, cam_ids)
+    )(places, turns, remain, cam_jac, cam_ids)
 
 
 def scalar_sums(received, residual, direction, damping, precond, owner_count):
@@ -432,7 +461,7 @@
     copies = lax.axis_size("pt")
     cam_jac = cam_jac.transpose(1, 0, 2)
     pt_jac = pt_jac.transpose(1, 0, 2)
-    payload, places = pack(
+    payload, places, turns = pack(
         owners.reshape(-1),
         valid_counts,
         direction,
@@ -445,7 +474,7 @@
     received = exchange(payload, "cam", owner_count)
     remain = points(received, pt_damping.reshape(-1, POINT_LOW))
     returned = exchange(remain, "cam", owner_count)
-    image_rows = cameras(places, returned, cam_jac, cam_ids, copies)
+    image_rows = cameras(places, turns, returned, cam_jac, cam_ids, copies)
     image_all = exchange(image_rows, "pt", copies)
     image, first_z, slope, scalars = scalar_sums(
         image_all, residual, direction, cam_damping, precond, owner_count

time: 91.2 us -> 89.6 us (0.982)
  waiting for transfers between devices: 19 us -> 17.7 us
    all_to_all x1, waiting for transfers between devices: 19 us -> 17.7 us  [exchange(): got = lax.all_to_all(sent, axis, split_axis=0, concat_axis=0, tiled=True)]
where the time goes in v4:
time: 89.6 us; the launch traced here: 89.2 us
  blocking collectives  48.5 us (54%)
  waiting for transfers between devices  17.7 us (20%)
  starting transfers between devices  11.6 us (13%)
  Pallas kernels  10.5 us (12%)
    all_to_all x3, blocking collectives, exchange(): got = lax.all_to_all(sent, axis, split_axis=0, concat_axis=0, tiled=True)  48.5 us
    all_to_all x1, waiting for transfers between devices, exchange(): got = lax.all_to_all(sent, axis, split_axis=0, concat_axis=0, tiled=True)  17.7 us
    all_to_all x1, starting transfers between devices, exchange(): got = lax.all_to_all(sent, axis, split_axis=0, concat_axis=0, tiled=True)  11.6 us
    pallas_call x1, Pallas kernels, points(): pl.pallas_call(point_kernel, out_shape=shape(slots * 2, LANES), in_specs=...  5.23 us
    pallas_call x1, Pallas kernels, pack(): pl.pallas_call(pack_kernel, out_shape=(pltpu.VMEM((owner_count * PER_OWNE...  2.3 us
    pallas_call x1, Pallas kernels, cameras(): pl.pallas_call(camera_kernel, out_shape=shape(copies * 18, LANES), in_spe...  2.06 us
  transfers between devices with their start and end apart: 1, of which 1 were waited for; matrix products, arithmetic and copies ran while one was open for 0% of the time, Pallas kernels for 0%

profile of v4, /device:TPU:1, one launch (start us, length us, event | category | flops | bytes accessed | tf_op | source)
XLA Modules:
  0.0 89.2 jit_solution(9170753114872160961)
XLA Ops:
  0.6 2.3 %pack_tiles.1 = (f32[1024,128]{1,0:T(8,128)}, f32[64,128]{1,0:T(8,128)S(1)}, f32[2,64,128]{2,1,0:T(8,128)S(1)}) custom-call(s32[64]{0:T(128)} %bitcast.27, s32[64]{0:T(128)} %refs_1_.1, f32[9,256]{1,0:T(8,128)} %direction.3, s32[64,128]{1,0:T(8,128)} %cam_ids.1, f32[18,64,128]{2,1,0:T(8,128)} %bitcast.17, f32[6,64,128]{2,1,0:T(8,128)} %bitcast.26, ...), custom_call_target="tpu_custom_call" | custom-call | tf_op jit(solution)/shard_map/pack_tiles/pallas_call | solution.py:361
  2.9 0.0 copy-start.7
  3.0 11.6 %all-to-all-start = ((f32[64,16,1,128]{3,1,2,0:T(8,128)}), f32[64,16,1,128]{3,1,2,0:T(8,128)S(1)}, u32[]{:S(2)}, u32[]{:S(2)}) async-start(f32[64,16,1,128]{3,1,2,0:T(8,128)} %bitcast.4), calls=%async_computation | async-start | bytes 1048576 | tf_op jit(solution)/shard_map/all_to_all | solution.py:442
  14.6 0.0 copy-done.7
  14.6 0.0 copy-start
  14.6 17.7 %all-to-all-done = f32[64,16,1,128]{3,1,2,0:T(8,128)S(1)} async-done(((f32[64,16,1,128]{3,1,2,0:T(8,128)}), f32[64,16,1,128]{3,1,2,0:T(8,128)S(1)}, u32[]{:S(2)}, u32[]{:S(2)}) %all-to-all-start) | async-done | bytes 524320 | tf_op jit(solution)/shard_map/all_to_all | solution.py:442
  32.3 5.2 %solve_points.1 = f32[256,128]{1,0:T(8,128)S(1)} custom-call(f32[1024,128]{1,0:T(8,128)S(1)} %bitcast.19, f32[8,256]{1,0:T(8,128)S(1)} %reshape.39.damping), custom_call_target="tpu_custom_call" | custom-call | tf_op jit(solution)/shard_map/solve_points/pallas_call | solution.py:384
  37.5 0.0 copy-start.2
  37.6 16.7 %all_to_all.20 = f32[64,4,1,128]{3,1,2,0:T(4,128)S(1)} all-to-all(f32[64,4,1,128]{3,1,2,0:T(4,128)S(1)} %bitcast.21), channel_id=1, replica_groups=mesh['cam'=64,'pt'=8] {'cam'}, dimensions={0} | all-to-all | bytes 262144 | tf_op jit(solution)/shard_map/all_to_all | solution.py:442
  54.2 0.0 copy-done
  54.2 0.0 copy-done.2
  54.2 2.1 %sum_cameras.1 = f32[144,128]{1,0:T(8,128)S(1)} custom-call(f32[64,128]{1,0:T(8,128)S(1)} %get-tuple-element.10.places, f32[2,64,128]{2,1,0:T(8,128)S(1)} %get-tuple-element.11.turns, f32[256,128]{1,0:T(8,128)S(1)} %bitcast.20, f32[18,64,128]{2,1,0:T(8,128)S(1)} %bitcast.18, s32[64,128]{1,0:T(8,128)S(1)} %copy-done.2), custom_call_target="tpu_custom_call" | custom-call | tf_op jit(solution)/shard_map/sum_cameras/pallas_call | solution.py:401
  56.3 0.0 copy-start.3
  56.3 0.0 copy-start.1
  56.3 0.0 copy-start.4
  56.3 0.0 copy-start.5
  56.3 17.2 %all_to_all.21 = f32[8,18,1,128]{3,2,1,0:T(1,128)S(1)} all-to-all(f32[8,18,1,128]{3,2,1,0:T(1,128)S(1)} %bitcast.22), channel_id=1, replica_groups=mesh['cam'=64,'pt'=8] {'pt'}, dimensions={0} | all-to-all | bytes 147456 | tf_op jit(solution)/shard_map/all_to_all | solution.py:442
  73.5 0.0 copy-done.3
  73.5 0.0 copy-done.5
  73.5 0.2 camera_scalars.1
  73.7 0.0 copy-start.6
  73.8 14.7 %all_to_all.22 = f32[64,1,1,128]{3,2,1,0:T(1,128)S(1)} all-to-all(f32[64,1,1,128]{3,2,1,0:T(1,128)S(1)} %bitcast.25), channel_id=1, replica_groups=mesh['cam'=64,'pt'=8] {'cam'}, dimensions={0} | all-to-all | bytes 65536 | tf_op jit(solution)/shard_map/all_to_all | solution.py:442
  88.5 0.0 copy-done.6
  88.5 0.7 update_vectors.1
  (3 shorter events, 0.0 us)
Async XLA Ops:
  2.9 11.7 %copy-start.7 = (f32[2048]{0:T(1024)S(1)}, f32[2048]{0:T(1024)}, u32[]{:S(2)}) copy-start(f32[2048]{0:T(1024)} %param.17) | copy-start | bytes 24580
  3.0 29.4 %all-to-all-start = ((f32[64,16,1,128]{3,1,2,0:T(8,128)}), f32[64,16,1,128]{3,1,2,0:T(8,128)S(1)}, u32[]{:S(2)}, u32[]{:S(2)}) async-start(f32[64,16,1,128]{3,1,2,0:T(8,128)} %bitcast.4), calls=%async_computation | async-start | bytes 1048576 | tf_op jit(solution)/shard_map/all_to_all | solution.py:442
  14.6 39.6 %copy-start = (f32[64,18,128]{2,0,1:T(8,128)S(1)}, f32[64,18,128]{2,0,1:T(8,128)}, u32[]{:S(2)}) copy-start(f32[64,18,128]{2,0,1:T(8,128)} %param.18) | copy-start | bytes 1769476
  37.5 16.7 %copy-start.2 = (s32[64,128]{1,0:T(8,128)S(1)}, s32[64,128]{1,0:T(8,128)}, u32[]{:S(2)}) copy-start(s32[64,128]{1,0:T(8,128)} %cam_ids.1) | copy-start | bytes 98308
  56.3 17.2 %copy-start.3 = (f32[81,256]{1,0:T(8,128)S(1)}, f32[81,256]{1,0:T(8,128)}, u32[]{:S(2)}) copy-start(f32[81,256]{1,0:T(8,128)} %precond.1) | copy-start | bytes 248836
  56.3 17.2 %copy-start.1 = (f32[9,256]{1,0:T(8,128)S(1)}, f32[9,256]{1,0:T(8,128)}, u32[]{:S(2)}) copy-start(f32[9,256]{1,0:T(8,128)} %direction.3) | copy-start | bytes 27652
  56.3 17.2 %copy-start.4 = (f32[9,256]{1,0:T(8,128)S(1)}, f32[9,256]{1,0:T(8,128)}, u32[]{:S(2)}) copy-start(f32[9,256]{1,0:T(8,128)} %residual.3) | copy-start | bytes 27652
  56.3 17.2 %copy-start.5 = (f32[9,256]{1,0:T(8,128)S(1)}, f32[9,256]{1,0:T(8,128)}, u32[]{:S(2)}) copy-start(f32[9,256]{1,0:T(8,128)} %damping.1) | copy-start | bytes 27652
  73.7 14.7 %copy-start.6 = (f32[9,256]{1,0:T(8,128)S(1)}, f32[9,256]{1,0:T(8,128)}, u32[]{:S(2)}) copy-start(f32[9,256]{1,0:T(8,128)} %solution_in.1) | copy-start | bytes 27652

commit v5 on v4

--- a/solution.py
+++ b/solution.py
@@ -15,9 +15,9 @@
 POINT_LOW = 256
 PARTS = 3
 CHUNK = 2
-PLACES = 4
+PLACES = 8
 WIDE = 2
-CAM_CHUNK = 4
+CAM_CHUNK = 2
 
 f32 = jnp.float32
 bf16 = jnp.bfloat16
@@ -49,6 +49,13 @@
 
 def one_hot(row_index, ids):
     return jnp.where(row_index == ids, jnp.ones((), bf16), jnp.zeros((), bf16))
+
+
+def by_upper(block, upper_row, uppers):
+    zero = jnp.zeros_like(block)
+    return jnp.concatenate(
+        [jnp.where(upper_row == jnp.asarray(h, bf16), block, zero) for h in range(uppers)], axis=0
+    )
 
 
 def spread(value, s, rows):
@@ -156,9 +163,8 @@
 def point_kernel(received, damping, remain, terms, sums, answers):
     slots = remain.shape[0] // 2
     groups = slots // GROUP
-    uppers = damping.shape[0]
+    uppers = damping.shape[0] // 2
     rows = GROUP * SLOT_ROWS
-    terms[...] = jnp.zeros(terms.shape, f32)
     sums[...] = jnp.zeros(sums.shape, f32)
     low_of_row = lax.broadcasted_iota(i32, (POINT_LOW, LANES), 0).astype(bf16)
 
@@ -183,15 +189,7 @@
                 at = ((place * CHUNK + k) * GROUP + s) * TERM_ROWS
                 block = terms[at : at + TERM_ROWS, :].astype(bf16)
                 upper_row = spread(upper, s, TERM_ROWS)
-                lefts.append(
-                    jnp.concatenate(
-                        [
-                            jnp.where(upper_row == jnp.asarray(h, bf16), block, jnp.zeros_like(block))
-                            for h in range(uppers)
-                        ],
-                        axis=0,
-                    )
-                )
+                lefts.append(by_upper(block, upper_row, uppers))
                 rights.append(one_hot(low_of_row, spread(lower, s, POINT_LOW)))
         return contract(jnp.concatenate(lefts, axis=1), jnp.concatenate(rights, axis=1))
 
@@ -203,7 +201,6 @@
                 sums[half] += added[:, half * LANES : (half + 1) * LANES]
 
     for half in range(2):
-        columns = slice(half * LANES, (half + 1) * LANES)
         total = []
         for term in range(9):
             pieces = [
@@ -211,9 +208,13 @@
                 for part in range(PARTS)
             ]
             total.append(pieces[0] + (pieces[1] + pieces[2]))
-        solved = solve_points(total[:3], total[3:], damping[:, columns])
+        solved = solve_points(total[:3], total[3:], damping[pl.ds(half, uppers, stride=2), :])
         for a in range(3):
-            answers[pl.ds((a * 2 + half) * uppers, uppers), :] = solved[a]
+            for h in range(uppers):
+                row = ((a * 2 + half) * uppers + h) * GROUP
+                answers[row : row + GROUP, :] = jnp.broadcast_to(
+                    solved[a][h : h + 1, :], (GROUP, LANES)
+                )
 
     @pl.loop(0, groups // WIDE)
     def _(step):
@@ -227,8 +228,8 @@
         for k in range(2 * uppers):
             h, half = k // 2, k % 2
             for a in range(3):
-                row = (a * 2 + half) * uppers + h
-                table = jnp.broadcast_to(answers[row : row + 1, :], (GROUP, LANES))
+                row = ((a * 2 + half) * uppers + h) * GROUP
+                table = answers[row : row + GROUP, :]
                 for w in range(WIDE):
                     value = lookup(table, lanes[w])
                     got[w][a] = value if k == 0 else jnp.where(chunks[w] == k, value, got[w][a])
@@ -247,10 +248,8 @@
 
 def camera_kernel(places, turns, remain, cam_jac, cam_ids, image, terms, stage):
     tiles = cam_ids.shape[0]
-    cams = 2 * LANES
     copies = image.shape[0] // 18
-    cam_of_row = lax.broadcasted_iota(i32, (cams, LANES), 0).astype(bf16)
-    terms[...] = jnp.zeros(terms.shape, f32)
+    low_of_row = lax.broadcasted_iota(i32, (LANES, LANES), 0).astype(bf16)
     chosen = places[...].astype(bf16)
     for r in range(2):
         high, middle, low = [
@@ -271,15 +270,18 @@
                 cam_jac[j, span, :] * rest[0] + cam_jac[9 + j, span, :] * rest[1] for j in range(9)
             ]
             store_terms(terms, values, group)
-            ids = cam_ids[span, :].astype(f32)
+            ids = cam_ids[span, :]
+            upper = (ids // LANES).astype(f32)
+            lower = (ids & (LANES - 1)).astype(f32)
             for s in range(GROUP):
                 at = (group * GROUP + s) * TERM_ROWS
-                lefts.append(terms[at : at + TERM_ROWS, :].astype(bf16))
-                rights.append(one_hot(cam_of_row, spread(ids, s, cams)))
+                block = terms[at : at + TERM_ROWS, :].astype(bf16)
+                lefts.append(by_upper(block, spread(upper, s, TERM_ROWS), 2))
+                rights.append(one_hot(low_of_row, spread(lower, s, LANES)))
         added = contract(jnp.concatenate(lefts, axis=1), jnp.concatenate(rights, axis=1))
         total = added if total is None else total + added
     for half in range(2):
-        terms[0:TERM_ROWS, :] = total[:, half * LANES : (half + 1) * LANES]
+        terms[0:TERM_ROWS, :] = total[half * TERM_ROWS : (half + 1) * TERM_ROWS, :]
         summed = terms[0:9, :] + (terms[9:18, :] + terms[18:27, :])
         for copy in range(copies):
             image[copy * 18 + half * 9 : copy * 18 + half * 9 + 9, :] = summed
@@ -380,7 +382,7 @@
 
 def points(received, damping):
     slots = received.shape[0] // SLOT_ROWS
-    uppers = damping.shape[0]
+    uppers = damping.shape[0] // 2
     return pl.pallas_call(
         point_kernel,
         out_shape=shape(slots * 2, LANES),
@@ -389,7 +391,7 @@
         scratch_shapes=[
             pltpu.VMEM((PLACES * CHUNK * GROUP * TERM_ROWS, LANES), f32),
             pltpu.VMEM((2, uppers * TERM_ROWS, LANES), f32),
-            pltpu.VMEM((6 * uppers, LANES), f32),
+            pltpu.VMEM((6 * uppers * GROUP, LANES), f32),
         ],
         compiler_params=LIMIT,
         name="solve_points",
@@ -472,7 +474,7 @@
         owner_count,
     )
     received = exchange(payload, "cam", owner_count)
-    remain = points(received, pt_damping.reshape(-1, POINT_LOW))
+    remain = points(received, pt_damping.reshape(-1, LANES))
     returned = exchange(remain, "cam", owner_count)
     image_rows = cameras(places, turns, returned, cam_jac, cam_ids, copies)
     image_all = exchange(image_rows, "pt", copies)

time: 89.6 us -> 87.8 us (0.980)
  blocking collectives: 48.5 us -> 77.7 us
  waiting for transfers between devices: 17.7 us -> 0 us
  starting transfers between devices: 11.6 us -> 0 us
  Pallas kernels: 10.5 us -> 8.97 us
    all_to_all x3 -> x4, blocking collectives: 48.5 us -> 77.7 us  [exchange(): got = lax.all_to_all(sent, axis, split_axis=0, concat_axis=0, tiled=True)]
    all_to_all x1 -> x0, waiting for transfers between devices: 17.7 us -> none  [exchange(): got = lax.all_to_all(sent, axis, split_axis=0, concat_axis=0, tiled=True)]
    all_to_all x1 -> x0, starting transfers between devices: 11.6 us -> none  [exchange(): got = lax.all_to_all(sent, axis, split_axis=0, concat_axis=0, tiled=True)]
  transfers between devices with their start and end apart: 1 -> 0, of which waited for: 1 -> 0; matrix products, arithmetic and copies ran while one was open for 0% -> 0% of each run, Pallas kernels for 0% -> 0%
where the time goes in v5:
time: 87.8 us; the launch traced here: 87.4 us
  blocking collectives  77.7 us (88%)
  Pallas kernels  8.97 us (10%)
    all_to_all x4, blocking collectives, exchange(): got = lax.all_to_all(sent, axis, split_axis=0, concat_axis=0, tiled=True)  77.7 us
    pallas_call x1, Pallas kernels, points(): pl.pallas_call(point_kernel, out_shape=shape(slots * 2, LANES), in_specs=...  4.99 us

profile of v5, /device:TPU:1, one launch (start us, length us, event | category | flops | bytes accessed | tf_op | source)
XLA Modules:
  0.0 87.4 jit_solution(5714890192382759892)
XLA Ops:
  0.6 1.5 %pack_tiles.1 = (f32[1024,128]{1,0:T(8,128)S(1)}, f32[64,128]{1,0:T(8,128)S(1)}, f32[2,64,128]{2,1,0:T(8,128)S(1)}) custom-call(s32[64]{0:T(128)} %bitcast.30, s32[64]{0:T(128)} %refs_1_.1, f32[9,256]{1,0:T(8,128)} %direction.3, s32[64,128]{1,0:T(8,128)} %cam_ids.1, f32[18,64,128]{2,1,0:T(8,128)} %bitcast.18, f32[6,64,128]{2,1,0:T(8,128)} %bitcast.29, ...), custom_call_target="tpu_custom_call" | custom-call | tf_op jit(solution)/shard_map/pack_tiles/pallas_call | solution.py:363
  2.2 0.0 copy-start.7
  2.2 29.1 %all_to_all.20 = f32[64,16,1,128]{3,1,2,0:T(8,128)S(1)} all-to-all(f32[64,16,1,128]{3,1,2,0:T(8,128)S(1)} %bitcast.22), channel_id=1, replica_groups=mesh['cam'=64,'pt'=8] {'cam'}, dimensions={0} | all-to-all | bytes 1048576 | tf_op jit(solution)/shard_map/all_to_all | solution.py:444
  31.3 0.0 copy-done.7
  31.3 5.0 %solve_points.1 = f32[256,128]{1,0:T(8,128)S(1)} custom-call(f32[1024,128]{1,0:T(8,128)S(1)} %bitcast.20, f32[16,128]{1,0:T(8,128)S(1)} %bitcast.28), custom_call_target="tpu_custom_call" | custom-call | tf_op jit(solution)/shard_map/solve_points/pallas_call | solution.py:386
  36.3 0.0 copy-start.2
  36.3 16.6 %all_to_all.21 = f32[64,4,1,128]{3,1,2,0:T(4,128)S(1)} all-to-all(f32[64,4,1,128]{3,1,2,0:T(4,128)S(1)} %bitcast.23), channel_id=1, replica_groups=mesh['cam'=64,'pt'=8] {'cam'}, dimensions={0} | all-to-all | bytes 262144 | tf_op jit(solution)/shard_map/all_to_all | solution.py:444
  53.0 0.0 copy-done
  53.0 0.0 copy-done.2
  53.0 1.6 %sum_cameras.1 = f32[144,128]{1,0:T(8,128)S(1)} custom-call(f32[64,128]{1,0:T(8,128)S(1)} %get-tuple-element.10.places, f32[2,64,128]{2,1,0:T(8,128)S(1)} %get-tuple-element.11.turns, f32[256,128]{1,0:T(8,128)S(1)} %bitcast.21, f32[18,64,128]{2,1,0:T(8,128)S(1)} %bitcast.19, s32[64,128]{1,0:T(8,128)S(1)} %copy-done.2), custom_call_target="tpu_custom_call" | custom-call | tf_op jit(solution)/shard_map/sum_cameras/pallas_call | solution.py:403
  54.5 0.0 copy-start.3
  54.5 0.0 copy-start.1
  54.5 0.0 copy-start.4
  54.6 0.0 copy-start.5
  54.6 17.2 %all_to_all.22 = f32[8,18,1,128]{3,2,1,0:T(1,128)S(1)} all-to-all(f32[8,18,1,128]{3,2,1,0:T(1,128)S(1)} %bitcast.24), channel_id=1, replica_groups=mesh['cam'=64,'pt'=8] {'pt'}, dimensions={0} | all-to-all | bytes 147456 | tf_op jit(solution)/shard_map/all_to_all | solution.py:444
  71.8 0.0 copy-done.3
  71.8 0.0 copy-done.1
  71.8 0.0 copy-done.4
  71.8 0.0 copy-done.5
  71.8 0.2 camera_scalars.1
  72.0 0.0 copy-start.6
  72.0 14.7 %all_to_all.23 = f32[64,1,1,128]{3,2,1,0:T(1,128)S(1)} all-to-all(f32[64,1,1,128]{3,2,1,0:T(1,128)S(1)} %bitcast.27), channel_id=1, replica_groups=mesh['cam'=64,'pt'=8] {'cam'}, dimensions={0} | all-to-all | bytes 65536 | tf_op jit(solution)/shard_map/all_to_all | solution.py:444
  86.7 0.0 copy-done.6
  86.7 0.7 update_vectors.1
  (1 shorter events, 0.0 us)
Async XLA Ops:
  2.2 29.2 %copy-start.7 = (f32[2048]{0:T(1024)S(1)}, f32[2048]{0:T(1024)}, u32[]{:S(2)}) copy-start(f32[2048]{0:T(1024)} %param.17) | copy-start | bytes 24580
  31.3 21.6 %copy-start = (f32[64,18,128]{2,0,1:T(8,128)S(1)}, f32[64,18,128]{2,0,1:T(8,128)}, u32[]{:S(2)}) copy-start(f32[64,18,128]{2,0,1:T(8,128)} %param.18) | copy-start | bytes 1769476
  36.3 16.7 %copy-start.2 = (s32[64,128]{1,0:T(8,128)S(1)}, s32[64,128]{1,0:T(8,128)}, u32[]{:S(2)}) copy-start(s32[64,128]{1,0:T(8,128)} %cam_ids.1) | copy-start | bytes 98308
  54.5 17.2 %copy-start.3 = (f32[81,256]{1,0:T(8,128)S(1)}, f32[81,256]{1,0:T(8,128)}, u32[]{:S(2)}) copy-start(f32[81,256]{1,0:T(8,128)} %precond.1) | copy-start | bytes 248836
  54.5 17.2 %copy-start.1 = (f32[9,256]{1,0:T(8,128)S(1)}, f32[9,256]{1,0:T(8,128)}, u32[]{:S(2)}) copy-start(f32[9,256]{1,0:T(8,128)} %direction.3) | copy-start | bytes 27652
  54.5 17.2 %copy-start.4 = (f32[9,256]{1,0:T(8,128)S(1)}, f32[9,256]{1,0:T(8,128)}, u32[]{:S(2)}) copy-start(f32[9,256]{1,0:T(8,128)} %residual.3) | copy-start | bytes 27652
  54.6 17.2 %copy-start.5 = (f32[9,256]{1,0:T(8,128)S(1)}, f32[9,256]{1,0:T(8,128)}, u32[]{:S(2)}) copy-start(f32[9,256]{1,0:T(8,128)} %damping.1) | copy-start | bytes 27652
  72.0 14.7 %copy-start.6 = (f32[9,256]{1,0:T(8,128)S(1)}, f32[9,256]{1,0:T(8,128)}, u32[]{:S(2)}) copy-start(f32[9,256]{1,0:T(8,128)} %solution_in.1) | copy-start | bytes 27652

commit v6 on v5

--- a/solution.py
+++ b/solution.py
@@ -16,7 +16,7 @@
 PARTS = 3
 CHUNK = 2
 PLACES = 8
-WIDE = 2
+WIDE = 8
 CAM_CHUNK = 2
 
 f32 = jnp.float32
@@ -44,7 +44,13 @@
     base = group * GROUP * TERM_ROWS
     for term, value in enumerate(values):
         for part, piece in enumerate(split(value)):
-            terms[pl.ds(base + part * 9 + term, GROUP, stride=TERM_ROWS), :] = piece
+            at = base + (part * 9 + term) * GROUP
+            terms[at : at + GROUP, :] = piece
+
+
+def slot_terms(terms, group, s):
+    rows = pl.ds(group * GROUP * TERM_ROWS + s, TERM_ROWS, stride=GROUP)
+    return terms[rows, :].astype(bf16)
 
 
 def one_hot(row_index, ids):
@@ -126,7 +132,8 @@
         values = [length, upper_row[0], upper_row[1], lower_row[0], lower_row[1]]
         values += [upper_row[2], lower_row[2], point_ids[span, :].astype(f32)]
         for r, value in enumerate(values):
-            stage[pl.ds(group * GROUP * SLOT_ROWS + r, GROUP, stride=SLOT_ROWS), :] = value
+            at = (group * SLOT_ROWS + r) * GROUP
+            stage[at : at + GROUP, :] = value
     slot_lane = lax.broadcasted_iota(i32, (1, places.shape[1]), 1)
     for tile in range(tiles):
         owner = owners[tile]
@@ -134,8 +141,9 @@
         seen[owner] = rank + 1
         slot = owner * PER_OWNER + rank
         places[tile : tile + 1, :] = jnp.where(slot_lane == slot, 1.0, 0.0)
+        at = tile // GROUP * GROUP * SLOT_ROWS + tile % GROUP
         payload[pl.ds(slot * SLOT_ROWS, SLOT_ROWS), :] = stage[
-            tile * SLOT_ROWS : (tile + 1) * SLOT_ROWS, :
+            pl.ds(at, SLOT_ROWS, stride=GROUP), :
         ]
 
 
@@ -186,8 +194,7 @@
                 values.append(first[a] * first[b] + second[a - 1] * second[b - 1])
             store_terms(terms, values, place * CHUNK + k)
             for s in range(GROUP):
-                at = ((place * CHUNK + k) * GROUP + s) * TERM_ROWS
-                block = terms[at : at + TERM_ROWS, :].astype(bf16)
+                block = slot_terms(terms, place * CHUNK + k, s)
                 upper_row = spread(upper, s, TERM_ROWS)
                 lefts.append(by_upper(block, upper_row, uppers))
                 rights.append(one_hot(low_of_row, spread(lower, s, POINT_LOW)))
@@ -225,13 +232,11 @@
         lanes = [value & (LANES - 1) for value in ids]
         chunks = [value // LANES for value in ids]
         got = [[None] * 3 for _ in range(WIDE)]
-        for k in range(2 * uppers):
-            h, half = k // 2, k % 2
+        for w in range(WIDE):
             for a in range(3):
-                row = ((a * 2 + half) * uppers + h) * GROUP
-                table = answers[row : row + GROUP, :]
-                for w in range(WIDE):
-                    value = lookup(table, lanes[w])
+                for k in range(2 * uppers):
+                    row = ((a * 2 + k % 2) * uppers + k // 2) * GROUP
+                    value = lookup(answers[row : row + GROUP, :], lanes[w])
                     got[w][a] = value if k == 0 else jnp.where(chunks[w] == k, value, got[w][a])
         for w, base in enumerate(bases):
             rows_of = [received[pl.ds(base + r, GROUP, stride=SLOT_ROWS), :] for r in range(7)]
@@ -274,8 +279,7 @@
             upper = (ids // LANES).astype(f32)
             lower = (ids & (LANES - 1)).astype(f32)
             for s in range(GROUP):
-                at = (group * GROUP + s) * TERM_ROWS
-                block = terms[at : at + TERM_ROWS, :].astype(bf16)
+                block = slot_terms(terms, group, s)
                 lefts.append(by_upper(block, spread(upper, s, TERM_ROWS), 2))
                 rights.append(one_hot(low_of_row, spread(lower, s, LANES)))
         added = contract(jnp.concatenate(lefts, axis=1), jnp.concatenate(rights, axis=1))

time: 87.8 us -> 85.8 us (0.977)
  Pallas kernels: 8.97 us -> 6.91 us
    pallas_call x1, Pallas kernels: 4.99 us -> 3.55 us  [points(): pl.pallas_call(point_kernel, out_shape=shape(slots * 2, LANES), in_specs=...]
where the time goes in v6:
time: 85.8 us; the launch traced here: 85.4 us
  blocking collectives  77.7 us (91%)
  Pallas kernels  6.91 us (8%)
    all_to_all x4, blocking collectives, exchange(): got = lax.all_to_all(sent, axis, split_axis=0, concat_axis=0, tiled=True)  77.7 us
    pallas_call x1, Pallas kernels, points(): pl.pallas_call(point_kernel, out_shape=shape(slots * 2, LANES), in_specs=...  3.55 us

profile of v6, /device:TPU:1, one launch (start us, length us, event | category | flops | bytes accessed | tf_op | source)
XLA Modules:
  0.0 85.4 jit_solution(8816434250513454527)
XLA Ops:
  0.6 1.5 %pack_tiles.1 = (f32[1024,128]{1,0:T(8,128)S(1)}, f32[64,128]{1,0:T(8,128)S(1)}, f32[2,64,128]{2,1,0:T(8,128)S(1)}) custom-call(s32[64]{0:T(128)} %bitcast.30, s32[64]{0:T(128)} %refs_1_.1, f32[9,256]{1,0:T(8,128)} %direction.3, s32[64,128]{1,0:T(8,128)} %cam_ids.1, f32[18,64,128]{2,1,0:T(8,128)} %bitcast.18, f32[6,64,128]{2,1,0:T(8,128)} %bitcast.29, ...), custom_call_target="tpu_custom_call" | custom-call | tf_op jit(solution)/shard_map/pack_tiles/pallas_call | solution.py:367
  2.2 0.0 copy-start.7
  2.2 29.1 %all_to_all.20 = f32[64,16,1,128]{3,1,2,0:T(8,128)S(1)} all-to-all(f32[64,16,1,128]{3,1,2,0:T(8,128)S(1)} %bitcast.22), channel_id=1, replica_groups=mesh['cam'=64,'pt'=8] {'cam'}, dimensions={0} | all-to-all | bytes 1048576 | tf_op jit(solution)/shard_map/all_to_all | solution.py:448
  31.3 0.0 copy-done.7
  31.3 3.6 %solve_points.1 = f32[256,128]{1,0:T(8,128)S(1)} custom-call(f32[1024,128]{1,0:T(8,128)S(1)} %bitcast.20, f32[16,128]{1,0:T(8,128)S(1)} %bitcast.28), custom_call_target="tpu_custom_call" | custom-call | tf_op jit(solution)/shard_map/solve_points/pallas_call | solution.py:390
  34.9 0.0 copy-start.2
  34.9 16.6 %all_to_all.21 = f32[64,4,1,128]{3,1,2,0:T(4,128)S(1)} all-to-all(f32[64,4,1,128]{3,1,2,0:T(4,128)S(1)} %bitcast.23), channel_id=1, replica_groups=mesh['cam'=64,'pt'=8] {'cam'}, dimensions={0} | all-to-all | bytes 262144 | tf_op jit(solution)/shard_map/all_to_all | solution.py:448
  51.5 0.0 copy-done
  51.5 0.0 copy-done.2
  51.5 0.9 %sum_cameras.1 = f32[144,128]{1,0:T(8,128)S(1)} custom-call(f32[64,128]{1,0:T(8,128)S(1)} %get-tuple-element.10.places, f32[2,64,128]{2,1,0:T(8,128)S(1)} %get-tuple-element.11.turns, f32[256,128]{1,0:T(8,128)S(1)} %bitcast.21, f32[18,64,128]{2,1,0:T(8,128)S(1)} %bitcast.19, s32[64,128]{1,0:T(8,128)S(1)} %copy-done.2), custom_call_target="tpu_custom_call" | custom-call | tf_op jit(solution)/shard_map/sum_cameras/pallas_call | solution.py:407
  52.5 0.0 copy-start.3
  52.5 0.0 copy-start.1
  52.5 0.0 copy-start.4
  52.5 0.0 copy-start.5
  52.5 17.2 %all_to_all.22 = f32[8,18,1,128]{3,2,1,0:T(1,128)S(1)} all-to-all(f32[8,18,1,128]{3,2,1,0:T(1,128)S(1)} %bitcast.24), channel_id=1, replica_groups=mesh['cam'=64,'pt'=8] {'pt'}, dimensions={0} | all-to-all | bytes 147456 | tf_op jit(solution)/shard_map/all_to_all | solution.py:448
  69.7 0.0 copy-done.3
  69.7 0.0 copy-done.1
  69.7 0.0 copy-done.4
  69.7 0.0 copy-done.5
  69.7 0.2 camera_scalars.1
  69.9 0.0 copy-start.6
  69.9 14.7 %all_to_all.23 = f32[64,1,1,128]{3,2,1,0:T(1,128)S(1)} all-to-all(f32[64,1,1,128]{3,2,1,0:T(1,128)S(1)} %bitcast.27), channel_id=1, replica_groups=mesh['cam'=64,'pt'=8] {'cam'}, dimensions={0} | all-to-all | bytes 65536 | tf_op jit(solution)/shard_map/all_to_all | solution.py:448
  84.6 0.0 copy-done.6
  84.6 0.7 update_vectors.1
  (1 shorter events, 0.0 us)
Async XLA Ops:
  2.2 29.2 %copy-start.7 = (f32[2048]{0:T(1024)S(1)}, f32[2048]{0:T(1024)}, u32[]{:S(2)}) copy-start(f32[2048]{0:T(1024)} %param.17) | copy-start | bytes 24580
  31.3 20.2 %copy-start = (f32[64,18,128]{2,0,1:T(8,128)S(1)}, f32[64,18,128]{2,0,1:T(8,128)}, u32[]{:S(2)}) copy-start(f32[64,18,128]{2,0,1:T(8,128)} %param.18) | copy-start | bytes 1769476
  34.9 16.7 %copy-start.2 = (s32[64,128]{1,0:T(8,128)S(1)}, s32[64,128]{1,0:T(8,128)}, u32[]{:S(2)}) copy-start(s32[64,128]{1,0:T(8,128)} %cam_ids.1) | copy-start | bytes 98308
  52.5 17.2 %copy-start.3 = (f32[81,256]{1,0:T(8,128)S(1)}, f32[81,256]{1,0:T(8,128)}, u32[]{:S(2)}) copy-start(f32[81,256]{1,0:T(8,128)} %precond.1) | copy-start | bytes 248836
  52.5 17.2 %copy-start.1 = (f32[9,256]{1,0:T(8,128)S(1)}, f32[9,256]{1,0:T(8,128)}, u32[]{:S(2)}) copy-start(f32[9,256]{1,0:T(8,128)} %direction.3) | copy-start | bytes 27652
  52.5 17.2 %copy-start.4 = (f32[9,256]{1,0:T(8,128)S(1)}, f32[9,256]{1,0:T(8,128)}, u32[]{:S(2)}) copy-start(f32[9,256]{1,0:T(8,128)} %residual.3) | copy-start | bytes 27652
  52.5 17.2 %copy-start.5 = (f32[9,256]{1,0:T(8,128)S(1)}, f32[9,256]{1,0:T(8,128)}, u32[]{:S(2)}) copy-start(f32[9,256]{1,0:T(8,128)} %damping.1) | copy-start | bytes 27652
  69.9 14.7 %copy-start.6 = (f32[9,256]{1,0:T(8,128)S(1)}, f32[9,256]{1,0:T(8,128)}, u32[]{:S(2)}) copy-start(f32[9,256]{1,0:T(8,128)} %solution_in.1) | copy-start | bytes 27652

commit v7 on v6

--- a/solution.py
+++ b/solution.py
@@ -14,9 +14,7 @@
 GROUP = 8
 POINT_LOW = 256
 PARTS = 3
-CHUNK = 2
-PLACES = 8
-WIDE = 8
+CHUNK = 4
 CAM_CHUNK = 2
 
 f32 = jnp.float32
@@ -173,13 +171,12 @@
     groups = slots // GROUP
     uppers = damping.shape[0] // 2
     rows = GROUP * SLOT_ROWS
-    sums[...] = jnp.zeros(sums.shape, f32)
     low_of_row = lax.broadcasted_iota(i32, (POINT_LOW, LANES), 0).astype(bf16)
 
-    def chunk(start, place):
+    def chunk(start):
         lefts, rights = [], []
-        for k in range(CHUNK):
-            base = (start + k) * rows
+        for group in range(start, start + CHUNK):
+            base = group * rows
             first = [received[pl.ds(base + r, GROUP, stride=SLOT_ROWS), :] for r in range(3)]
             second = [received[pl.ds(base + 3 + r, GROUP, stride=SLOT_ROWS), :] for r in range(2)]
             err0 = received[pl.ds(base + 5, GROUP, stride=SLOT_ROWS), :]
@@ -192,20 +189,19 @@
             values += [first[0] * first[a] for a in range(3)]
             for a, b in ((1, 1), (1, 2), (2, 2)):
                 values.append(first[a] * first[b] + second[a - 1] * second[b - 1])
-            store_terms(terms, values, place * CHUNK + k)
+            store_terms(terms, values, group)
             for s in range(GROUP):
-                block = slot_terms(terms, place * CHUNK + k, s)
+                block = slot_terms(terms, group, s)
                 upper_row = spread(upper, s, TERM_ROWS)
                 lefts.append(by_upper(block, upper_row, uppers))
                 rights.append(one_hot(low_of_row, spread(lower, s, POINT_LOW)))
         return contract(jnp.concatenate(lefts, axis=1), jnp.concatenate(rights, axis=1))
 
-    @pl.loop(0, groups // (CHUNK * PLACES))
-    def _(step):
-        for place in range(PLACES):
-            added = chunk((step * PLACES + place) * CHUNK, place)
-            for half in range(2):
-                sums[half] += added[:, half * LANES : (half + 1) * LANES]
+    total = chunk(0)
+    for start in range(CHUNK, groups, CHUNK):
+        total = total + chunk(start)
+    for half in range(2):
+        sums[half] = total[:, half * LANES : (half + 1) * LANES]
 
     for half in range(2):
         total = []
@@ -223,32 +219,25 @@
                     solved[a][h : h + 1, :], (GROUP, LANES)
                 )
 
-    @pl.loop(0, groups // WIDE)
-    def _(step):
-        bases = [(step * WIDE + w) * rows for w in range(WIDE)]
-        ids = [
-            received[pl.ds(base + 7, GROUP, stride=SLOT_ROWS), :].astype(i32) for base in bases
+    for group in range(groups):
+        base = group * rows
+        row_of = [received[pl.ds(base + r, GROUP, stride=SLOT_ROWS), :] for r in range(SLOT_ROWS)]
+        ids = row_of[7].astype(i32)
+        lane = ids & (LANES - 1)
+        chunk_of = ids // LANES
+        y = []
+        for a in range(3):
+            for k in range(2 * uppers):
+                row = ((a * 2 + k % 2) * uppers + k // 2) * GROUP
+                value = lookup(answers[row : row + GROUP, :], lane)
+                got = value if k == 0 else jnp.where(chunk_of == k, value, got)
+            y.append(got)
+        images = [
+            row_of[0] * y[0] + (row_of[1] * y[1] + row_of[2] * y[2]),
+            row_of[3] * y[1] + row_of[4] * y[2],
         ]
-        lanes = [value & (LANES - 1) for value in ids]
-        chunks = [value // LANES for value in ids]
-        got = [[None] * 3 for _ in range(WIDE)]
-        for w in range(WIDE):
-            for a in range(3):
-                for k in range(2 * uppers):
-                    row = ((a * 2 + k % 2) * uppers + k // 2) * GROUP
-                    value = lookup(answers[row : row + GROUP, :], lanes[w])
-                    got[w][a] = value if k == 0 else jnp.where(chunks[w] == k, value, got[w][a])
-        for w, base in enumerate(bases):
-            rows_of = [received[pl.ds(base + r, GROUP, stride=SLOT_ROWS), :] for r in range(7)]
-            y = got[w]
-            images = [
-                rows_of[0] * y[0] + (rows_of[1] * y[1] + rows_of[2] * y[2]),
-                rows_of[3] * y[1] + rows_of[4] * y[2],
-            ]
-            for r in range(2):
-                remain[pl.ds((step * WIDE + w) * 2 * GROUP + r, GROUP, stride=2), :] = (
-                    rows_of[5 + r] - images[r]
-                )
+        for r in range(2):
+            remain[pl.ds(group * 2 * GROUP + r, GROUP, stride=2), :] = row_of[5 + r] - images[r]
 
 
 def camera_kernel(places, turns, remain, cam_jac, cam_ids, image, terms, stage):
@@ -351,7 +340,6 @@
     new_direction[...] = first_z[...] - alpha * slope[...] + (rz1 / rz) * way
 
 
-SMEM = pl.BlockSpec(memory_space=pltpu.SMEM)
 VMEM = pl.BlockSpec(memory_space=pltpu.VMEM)
 LIMIT = pltpu.CompilerParams(vmem_limit_bytes=32 * 1024 * 1024)
 
@@ -393,7 +381,7 @@
         in_specs=[VMEM] * 2,
         out_specs=VMEM,
         scratch_shapes=[
-            pltpu.VMEM((PLACES * CHUNK * GROUP * TERM_ROWS, LANES), f32),
+            pltpu.VMEM((slots * TERM_ROWS, LANES), f32),
             pltpu.VMEM((2, uppers * TERM_ROWS, LANES), f32),
             pltpu.VMEM((6 * uppers * GROUP, LANES), f32),
         ],

time: 85.8 us -> 85.7 us (level)
  no operation moved by 1% of the time
where the time goes in v7:
time: 85.7 us; the launch traced here: 85.3 us
  blocking collectives  77.7 us (91%)
  Pallas kernels  6.85 us (8%)
    all_to_all x4, blocking collectives, exchange(): got = lax.all_to_all(sent, axis, split_axis=0, concat_axis=0, tiled=True)  77.7 us
    pallas_call x1, Pallas kernels, points(): pl.pallas_call(point_kernel, out_shape=shape(slots * 2, LANES), in_specs=...  3.49 us

profile of v7, /device:TPU:1, one launch (start us, length us, event | category | flops | bytes accessed | tf_op | source)
XLA Modules:
  0.0 85.3 jit_solution(11019429230939968154)
XLA Ops:
  0.6 1.5 %pack_tiles.1 = (f32[1024,128]{1,0:T(8,128)S(1)}, f32[64,128]{1,0:T(8,128)S(1)}, f32[2,64,128]{2,1,0:T(8,128)S(1)}) custom-call(s32[64]{0:T(128)} %bitcast.30, s32[64]{0:T(128)} %refs_1_.1, f32[9,256]{1,0:T(8,128)} %direction.3, s32[64,128]{1,0:T(8,128)} %cam_ids.1, f32[18,64,128]{2,1,0:T(8,128)} %bitcast.18, f32[6,64,128]{2,1,0:T(8,128)} %bitcast.29, ...), custom_call_target="tpu_custom_call" | custom-call | tf_op jit(solution)/shard_map/pack_tiles/pallas_call | solution.py:355
  2.2 0.0 copy-start.7
  2.2 29.1 %all_to_all.20 = f32[64,16,1,128]{3,1,2,0:T(8,128)S(1)} all-to-all(f32[64,16,1,128]{3,1,2,0:T(8,128)S(1)} %bitcast.22), channel_id=1, replica_groups=mesh['cam'=64,'pt'=8] {'cam'}, dimensions={0} | all-to-all | bytes 1048576 | tf_op jit(solution)/shard_map/all_to_all | solution.py:436
  31.3 0.0 copy-done.7
  31.3 3.5 %solve_points.1 = f32[256,128]{1,0:T(8,128)S(1)} custom-call(f32[1024,128]{1,0:T(8,128)S(1)} %bitcast.20, f32[16,128]{1,0:T(8,128)S(1)} %bitcast.28), custom_call_target="tpu_custom_call" | custom-call | tf_op jit(solution)/shard_map/solve_points/pallas_call | solution.py:378
  34.8 0.0 copy-start.2
  34.8 16.6 %all_to_all.21 = f32[64,4,1,128]{3,1,2,0:T(4,128)S(1)} all-to-all(f32[64,4,1,128]{3,1,2,0:T(4,128)S(1)} %bitcast.23), channel_id=1, replica_groups=mesh['cam'=64,'pt'=8] {'cam'}, dimensions={0} | all-to-all | bytes 262144 | tf_op jit(solution)/shard_map/all_to_all | solution.py:436
  51.5 0.0 copy-done
  51.5 0.0 copy-done.2
  51.5 0.9 %sum_cameras.1 = f32[144,128]{1,0:T(8,128)S(1)} custom-call(f32[64,128]{1,0:T(8,128)S(1)} %get-tuple-element.10.places, f32[2,64,128]{2,1,0:T(8,128)S(1)} %get-tuple-element.11.turns, f32[256,128]{1,0:T(8,128)S(1)} %bitcast.21, f32[18,64,128]{2,1,0:T(8,128)S(1)} %bitcast.19, s32[64,128]{1,0:T(8,128)S(1)} %copy-done.2), custom_call_target="tpu_custom_call" | custom-call | tf_op jit(solution)/shard_map/sum_cameras/pallas_call | solution.py:395
  52.4 0.0 copy-start.3
  52.4 0.0 copy-start.1
  52.4 0.0 copy-start.4
  52.5 0.0 copy-start.5
  52.5 17.2 %all_to_all.22 = f32[8,18,1,128]{3,2,1,0:T(1,128)S(1)} all-to-all(f32[8,18,1,128]{3,2,1,0:T(1,128)S(1)} %bitcast.24), channel_id=1, replica_groups=mesh['cam'=64,'pt'=8] {'pt'}, dimensions={0} | all-to-all | bytes 147456 | tf_op jit(solution)/shard_map/all_to_all | solution.py:436
  69.7 0.0 copy-done.3
  69.7 0.0 copy-done.1
  69.7 0.0 copy-done.4
  69.7 0.0 copy-done.5
  69.7 0.2 camera_scalars.1
  69.9 0.0 copy-start.6
  69.9 14.7 %all_to_all.23 = f32[64,1,1,128]{3,2,1,0:T(1,128)S(1)} all-to-all(f32[64,1,1,128]{3,2,1,0:T(1,128)S(1)} %bitcast.27), channel_id=1, replica_groups=mesh['cam'=64,'pt'=8] {'cam'}, dimensions={0} | all-to-all | bytes 65536 | tf_op jit(solution)/shard_map/all_to_all | solution.py:436
  84.6 0.0 copy-done.6
  84.6 0.7 update_vectors.1
  (1 shorter events, 0.0 us)
Async XLA Ops:
  2.2 29.2 %copy-start.7 = (f32[2048]{0:T(1024)S(1)}, f32[2048]{0:T(1024)}, u32[]{:S(2)}) copy-start(f32[2048]{0:T(1024)} %param.17) | copy-start | bytes 24580
  31.3 20.2 %copy-start = (f32[64,18,128]{2,0,1:T(8,128)S(1)}, f32[64,18,128]{2,0,1:T(8,128)}, u32[]{:S(2)}) copy-start(f32[64,18,128]{2,0,1:T(8,128)} %param.18) | copy-start | bytes 1769476
  34.8 16.7 %copy-start.2 = (s32[64,128]{1,0:T(8,128)S(1)}, s32[64,128]{1,0:T(8,128)}, u32[]{:S(2)}) copy-start(s32[64,128]{1,0:T(8,128)} %cam_ids.1) | copy-start | bytes 98308
  52.4 17.2 %copy-start.3 = (f32[81,256]{1,0:T(8,128)S(1)}, f32[81,256]{1,0:T(8,128)}, u32[]{:S(2)}) copy-start(f32[81,256]{1,0:T(8,128)} %precond.1) | copy-start | bytes 248836
  52.4 17.2 %copy-start.1 = (f32[9,256]{1,0:T(8,128)S(1)}, f32[9,256]{1,0:T(8,128)}, u32[]{:S(2)}) copy-start(f32[9,256]{1,0:T(8,128)} %direction.3) | copy-start | bytes 27652
  52.4 17.2 %copy-start.4 = (f32[9,256]{1,0:T(8,128)S(1)}, f32[9,256]{1,0:T(8,128)}, u32[]{:S(2)}) copy-start(f32[9,256]{1,0:T(8,128)} %residual.3) | copy-start | bytes 27652
  52.5 17.2 %copy-start.5 = (f32[9,256]{1,0:T(8,128)S(1)}, f32[9,256]{1,0:T(8,128)}, u32[]{:S(2)}) copy-start(f32[9,256]{1,0:T(8,128)} %damping.1) | copy-start | bytes 27652
  69.9 14.7 %copy-start.6 = (f32[9,256]{1,0:T(8,128)S(1)}, f32[9,256]{1,0:T(8,128)}, u32[]{:S(2)}) copy-start(f32[9,256]{1,0:T(8,128)} %solution_in.1) | copy-start | bytes 27652

commit v8 on v7

--- a/solution.py
+++ b/solution.py
@@ -14,6 +14,7 @@
 GROUP = 8
 POINT_LOW = 256
 PARTS = 3
+PIECES = 2
 CHUNK = 4
 CAM_CHUNK = 2
 
@@ -166,12 +167,19 @@
     )
 
 
-def point_kernel(received, damping, remain, terms, sums, answers):
+def point_kernel(received, damping, remain, terms, turned, answers):
     slots = remain.shape[0] // 2
     groups = slots // GROUP
     uppers = damping.shape[0] // 2
     rows = GROUP * SLOT_ROWS
-    low_of_row = lax.broadcasted_iota(i32, (POINT_LOW, LANES), 0).astype(bf16)
+    low_of_lane = lax.broadcasted_iota(i32, (LANES, POINT_LOW), 1).astype(bf16)
+    upper_of_row = lax.broadcasted_iota(i32, (uppers, LANES), 0)
+    ids_of = [
+        received[pl.ds(group * rows + 7, GROUP, stride=SLOT_ROWS), :].astype(i32)
+        for group in range(groups)
+    ]
+    lows = jnp.concatenate([(ids & (POINT_LOW - 1)).astype(f32) for ids in ids_of], axis=0)
+    turned[...] = lows.T
 
     def chunk(start):
         lefts, rights = [], []
@@ -181,9 +189,7 @@
             second = [received[pl.ds(base + 3 + r, GROUP, stride=SLOT_ROWS), :] for r in range(2)]
             err0 = received[pl.ds(base + 5, GROUP, stride=SLOT_ROWS), :]
             err1 = received[pl.ds(base + 6, GROUP, stride=SLOT_ROWS), :]
-            ids = received[pl.ds(base + 7, GROUP, stride=SLOT_ROWS), :].astype(i32)
-            upper = (ids // POINT_LOW).astype(f32)
-            lower = (ids & (POINT_LOW - 1)).astype(f32)
+            upper = ids_of[group] // POINT_LOW
             values = [first[0] * err0]
             values += [first[a] * err0 + second[a - 1] * err1 for a in (1, 2)]
             values += [first[0] * first[a] for a in range(3)]
@@ -191,26 +197,41 @@
                 values.append(first[a] * first[b] + second[a - 1] * second[b - 1])
             store_terms(terms, values, group)
             for s in range(GROUP):
-                block = slot_terms(terms, group, s)
-                upper_row = spread(upper, s, TERM_ROWS)
-                lefts.append(by_upper(block, upper_row, uppers))
-                rights.append(one_hot(low_of_row, spread(lower, s, POINT_LOW)))
-        return contract(jnp.concatenate(lefts, axis=1), jnp.concatenate(rights, axis=1))
-
-    total = chunk(0)
+                mask = upper_of_row == jnp.broadcast_to(upper[s : s + 1, :], (uppers, LANES))
+                pieces = []
+                for r in range(9 * PIECES):
+                    at = group * GROUP * TERM_ROWS + r * GROUP + s
+                    pieces.append(
+                        jnp.where(mask, jnp.broadcast_to(terms[at : at + 1, :], (uppers, LANES)), 0.0)
+                    )
+                lefts.append(jnp.concatenate(pieces, axis=0).astype(bf16))
+                slot = group * GROUP + s
+                column = jnp.broadcast_to(turned[:, slot : slot + 1], (LANES, LANES)).astype(bf16)
+                rights.append(
+                    jnp.concatenate(
+                        [one_hot(low_of_lane[:, h * LANES : (h + 1) * LANES], column) for h in range(2)],
+                        axis=1,
+                    )
+                )
+        return lax.dot_general(
+            jnp.concatenate(lefts, axis=1),
+            jnp.concatenate(rights, axis=0),
+            (((1,), (0,)), ((), ())),
+            preferred_element_type=f32,
+        )
+
+    whole = chunk(0)
     for start in range(CHUNK, groups, CHUNK):
-        total = total + chunk(start)
-    for half in range(2):
-        sums[half] = total[:, half * LANES : (half + 1) * LANES]
+        whole = whole + chunk(start)
 
     for half in range(2):
         total = []
         for term in range(9):
-            pieces = [
-                sums[half, pl.ds(part * 9 + term, uppers, stride=TERM_ROWS), :]
-                for part in range(PARTS)
+            parts = [
+                whole[(p * 9 + term) * uppers : (p * 9 + term + 1) * uppers, half * LANES : (half + 1) * LANES]
+                for p in range(PIECES)
             ]
-            total.append(pieces[0] + (pieces[1] + pieces[2]))
+            total.append(parts[0] + sum(parts[2:], parts[1]))
         solved = solve_points(total[:3], total[3:], damping[pl.ds(half, uppers, stride=2), :])
         for a in range(3):
             for h in range(uppers):
@@ -382,7 +403,7 @@
         out_specs=VMEM,
         scratch_shapes=[
             pltpu.VMEM((slots * TERM_ROWS, LANES), f32),
-            pltpu.VMEM((2, uppers * TERM_ROWS, LANES), f32),
+            pltpu.VMEM((LANES, slots), f32),
             pltpu.VMEM((6 * uppers * GROUP, LANES), f32),
         ],
         compiler_params=LIMIT,

time: 85.7 us -> 85.5 us (level)
  no operation moved by 1% of the time
where the time goes in v8:
time: 85.5 us; the launch traced here: 85.1 us
  blocking collectives  77.7 us (91%)
  Pallas kernels  6.61 us (8%)
    all_to_all x4, blocking collectives, exchange(): got = lax.all_to_all(sent, axis, split_axis=0, concat_axis=0, tiled=True)  77.7 us
    pallas_call x1, Pallas kernels, points(): pl.pallas_call(point_kernel, out_shape=shape(slots * 2, LANES), in_specs=...  3.25 us

profile of v8, /device:TPU:1, one launch (start us, length us, event | category | flops | bytes accessed | tf_op | source)
XLA Modules:
  0.0 85.1 jit_solution(1995899207815461485)
XLA Ops:
  0.6 1.5 %pack_tiles.1 = (f32[1024,128]{1,0:T(8,128)S(1)}, f32[64,128]{1,0:T(8,128)S(1)}, f32[2,64,128]{2,1,0:T(8,128)S(1)}) custom-call(s32[64]{0:T(128)} %bitcast.30, s32[64]{0:T(128)} %refs_1_.1, f32[9,256]{1,0:T(8,128)} %direction.3, s32[64,128]{1,0:T(8,128)} %cam_ids.1, f32[18,64,128]{2,1,0:T(8,128)} %bitcast.18, f32[6,64,128]{2,1,0:T(8,128)} %bitcast.29, ...), custom_call_target="tpu_custom_call" | custom-call | tf_op jit(solution)/shard_map/pack_tiles/pallas_call | solution.py:376
  2.2 0.0 copy-start.7
  2.2 29.1 %all_to_all.20 = f32[64,16,1,128]{3,1,2,0:T(8,128)S(1)} all-to-all(f32[64,16,1,128]{3,1,2,0:T(8,128)S(1)} %bitcast.22), channel_id=1, replica_groups=mesh['cam'=64,'pt'=8] {'cam'}, dimensions={0} | all-to-all | bytes 1048576 | tf_op jit(solution)/shard_map/all_to_all | solution.py:457
  31.3 0.0 copy-done.7
  31.3 3.3 %solve_points.1 = f32[256,128]{1,0:T(8,128)S(1)} custom-call(f32[1024,128]{1,0:T(8,128)S(1)} %bitcast.20, f32[16,128]{1,0:T(8,128)S(1)} %bitcast.28), custom_call_target="tpu_custom_call" | custom-call | tf_op jit(solution)/shard_map/solve_points/pallas_call | solution.py:399
  34.6 0.0 copy-start.2
  34.6 16.6 %all_to_all.21 = f32[64,4,1,128]{3,1,2,0:T(4,128)S(1)} all-to-all(f32[64,4,1,128]{3,1,2,0:T(4,128)S(1)} %bitcast.23), channel_id=1, replica_groups=mesh['cam'=64,'pt'=8] {'cam'}, dimensions={0} | all-to-all | bytes 262144 | tf_op jit(solution)/shard_map/all_to_all | solution.py:457
  51.2 0.0 copy-done
  51.2 0.0 copy-done.2
  51.2 0.9 %sum_cameras.1 = f32[144,128]{1,0:T(8,128)S(1)} custom-call(f32[64,128]{1,0:T(8,128)S(1)} %get-tuple-element.10.places, f32[2,64,128]{2,1,0:T(8,128)S(1)} %get-tuple-element.11.turns, f32[256,128]{1,0:T(8,128)S(1)} %bitcast.21, f32[18,64,128]{2,1,0:T(8,128)S(1)} %bitcast.19, s32[64,128]{1,0:T(8,128)S(1)} %copy-done.2), custom_call_target="tpu_custom_call" | custom-call | tf_op jit(solution)/shard_map/sum_cameras/pallas_call | solution.py:416
  52.2 0.0 copy-start.3
  52.2 0.0 copy-start.1
  52.2 0.0 copy-start.4
  52.2 0.0 copy-start.5
  52.2 17.2 %all_to_all.22 = f32[8,18,1,128]{3,2,1,0:T(1,128)S(1)} all-to-all(f32[8,18,1,128]{3,2,1,0:T(1,128)S(1)} %bitcast.24), channel_id=1, replica_groups=mesh['cam'=64,'pt'=8] {'pt'}, dimensions={0} | all-to-all | bytes 147456 | tf_op jit(solution)/shard_map/all_to_all | solution.py:457
  69.4 0.0 copy-done.3
  69.4 0.0 copy-done.1
  69.4 0.0 copy-done.4
  69.4 0.0 copy-done.5
  69.4 0.2 camera_scalars.1
  69.6 0.0 copy-start.6
  69.6 14.7 %all_to_all.23 = f32[64,1,1,128]{3,2,1,0:T(1,128)S(1)} all-to-all(f32[64,1,1,128]{3,2,1,0:T(1,128)S(1)} %bitcast.27), channel_id=1, replica_groups=mesh['cam'=64,'pt'=8] {'cam'}, dimensions={0} | all-to-all | bytes 65536 | tf_op jit(solution)/shard_map/all_to_all | solution.py:457
  84.3 0.0 copy-done.6
  84.3 0.7 update_vectors.1
  (1 shorter events, 0.0 us)
Async XLA Ops:
  2.2 29.2 %copy-start.7 = (f32[2048]{0:T(1024)S(1)}, f32[2048]{0:T(1024)}, u32[]{:S(2)}) copy-start(f32[2048]{0:T(1024)} %param.17) | copy-start | bytes 24580
  31.3 19.9 %copy-start = (f32[64,18,128]{2,0,1:T(8,128)S(1)}, f32[64,18,128]{2,0,1:T(8,128)}, u32[]{:S(2)}) copy-start(f32[64,18,128]{2,0,1:T(8,128)} %param.18) | copy-start | bytes 1769476
  34.6 16.7 %copy-start.2 = (s32[64,128]{1,0:T(8,128)S(1)}, s32[64,128]{1,0:T(8,128)}, u32[]{:S(2)}) copy-start(s32[64,128]{1,0:T(8,128)} %cam_ids.1) | copy-start | bytes 98308
  52.2 17.2 %copy-start.3 = (f32[81,256]{1,0:T(8,128)S(1)}, f32[81,256]{1,0:T(8,128)}, u32[]{:S(2)}) copy-start(f32[81,256]{1,0:T(8,128)} %precond.1) | copy-start | bytes 248836
  52.2 17.2 %copy-start.1 = (f32[9,256]{1,0:T(8,128)S(1)}, f32[9,256]{1,0:T(8,128)}, u32[]{:S(2)}) copy-start(f32[9,256]{1,0:T(8,128)} %direction.3) | copy-start | bytes 27652
  52.2 17.2 %copy-start.4 = (f32[9,256]{1,0:T(8,128)S(1)}, f32[9,256]{1,0:T(8,128)}, u32[]{:S(2)}) copy-start(f32[9,256]{1,0:T(8,128)} %residual.3) | copy-start | bytes 27652
  52.2 17.2 %copy-start.5 = (f32[9,256]{1,0:T(8,128)S(1)}, f32[9,256]{1,0:T(8,128)}, u32[]{:S(2)}) copy-start(f32[9,256]{1,0:T(8,128)} %damping.1) | copy-start | bytes 27652
  69.6 14.7 %copy-start.6 = (f32[9,256]{1,0:T(8,128)S(1)}, f32[9,256]{1,0:T(8,128)}, u32[]{:S(2)}) copy-start(f32[9,256]{1,0:T(8,128)} %solution_in.1) | copy-start | bytes 27652

commit v9 on v7

--- a/solution.py
+++ b/solution.py
@@ -197,6 +197,7 @@
                 rights.append(one_hot(low_of_row, spread(lower, s, POINT_LOW)))
         return contract(jnp.concatenate(lefts, axis=1), jnp.concatenate(rights, axis=1))
 
+    tables = {}
     total = chunk(0)
     for start in range(CHUNK, groups, CHUNK):
         total = total + chunk(start)
@@ -214,10 +215,7 @@
         solved = solve_points(total[:3], total[3:], damping[pl.ds(half, uppers, stride=2), :])
         for a in range(3):
             for h in range(uppers):
-                row = ((a * 2 + half) * uppers + h) * GROUP
-                answers[row : row + GROUP, :] = jnp.broadcast_to(
-                    solved[a][h : h + 1, :], (GROUP, LANES)
-                )
+                tables[a, 2 * h + half] = jnp.broadcast_to(solved[a][h : h + 1, :], (GROUP, LANES))
 
     for group in range(groups):
         base = group * rows
@@ -228,8 +226,7 @@
         y = []
         for a in range(3):
             for k in range(2 * uppers):
-                row = ((a * 2 + k % 2) * uppers + k // 2) * GROUP
-                value = lookup(answers[row : row + GROUP, :], lane)
+                value = lookup(tables[a, k], lane)
                 got = value if k == 0 else jnp.where(chunk_of == k, value, got)
             y.append(got)
         images = [

time: 85.7 us -> 85.7 us (level)
  no operation moved by 1% of the time
where the time goes in v9:
time: 85.7 us; the launch traced here: 85.3 us
  blocking collectives  77.7 us (91%)
  Pallas kernels  6.85 us (8%)
    all_to_all x4, blocking collectives, exchange(): got = lax.all_to_all(sent, axis, split_axis=0, concat_axis=0, tiled=True)  77.7 us
    pallas_call x1, Pallas kernels, points(): pl.pallas_call(point_kernel, out_shape=shape(slots * 2, LANES), in_specs=...  3.49 us

profile of v9, /device:TPU:1, one launch (start us, length us, event | category | flops | bytes accessed | tf_op | source)
XLA Modules:
  0.0 85.3 jit_solution(11019429230939968154)
XLA Ops:
  0.6 1.5 %pack_tiles.1 = (f32[1024,128]{1,0:T(8,128)S(1)}, f32[64,128]{1,0:T(8,128)S(1)}, f32[2,64,128]{2,1,0:T(8,128)S(1)}) custom-call(s32[64]{0:T(128)} %bitcast.30, s32[64]{0:T(128)} %refs_1_.1, f32[9,256]{1,0:T(8,128)} %direction.3, s32[64,128]{1,0:T(8,128)} %cam_ids.1, f32[18,64,128]{2,1,0:T(8,128)} %bitcast.18, f32[6,64,128]{2,1,0:T(8,128)} %bitcast.29, ...), custom_call_target="tpu_custom_call" | custom-call | tf_op jit(solution)/shard_map/pack_tiles/pallas_call | solution.py:352
  2.2 0.0 copy-start.7
  2.2 29.1 %all_to_all.20 = f32[64,16,1,128]{3,1,2,0:T(8,128)S(1)} all-to-all(f32[64,16,1,128]{3,1,2,0:T(8,128)S(1)} %bitcast.22), channel_id=1, replica_groups=mesh['cam'=64,'pt'=8] {'cam'}, dimensions={0} | all-to-all | bytes 1048576 | tf_op jit(solution)/shard_map/all_to_all | solution.py:433
  31.3 0.0 copy-done.7
  31.3 3.5 %solve_points.1 = f32[256,128]{1,0:T(8,128)S(1)} custom-call(f32[1024,128]{1,0:T(8,128)S(1)} %bitcast.20, f32[16,128]{1,0:T(8,128)S(1)} %bitcast.28), custom_call_target="tpu_custom_call" | custom-call | tf_op jit(solution)/shard_map/solve_points/pallas_call | solution.py:375
  34.8 0.0 copy-start.2
  34.8 16.6 %all_to_all.21 = f32[64,4,1,128]{3,1,2,0:T(4,128)S(1)} all-to-all(f32[64,4,1,128]{3,1,2,0:T(4,128)S(1)} %bitcast.23), channel_id=1, replica_groups=mesh['cam'=64,'pt'=8] {'cam'}, dimensions={0} | all-to-all | bytes 262144 | tf_op jit(solution)/shard_map/all_to_all | solution.py:433
  51.5 0.0 copy-done
  51.5 0.0 copy-done.2
  51.5 0.9 %sum_cameras.1 = f32[144,128]{1,0:T(8,128)S(1)} custom-call(f32[64,128]{1,0:T(8,128)S(1)} %get-tuple-element.10.places, f32[2,64,128]{2,1,0:T(8,128)S(1)} %get-tuple-element.11.turns, f32[256,128]{1,0:T(8,128)S(1)} %bitcast.21, f32[18,64,128]{2,1,0:T(8,128)S(1)} %bitcast.19, s32[64,128]{1,0:T(8,128)S(1)} %copy-done.2), custom_call_target="tpu_custom_call" | custom-call | tf_op jit(solution)/shard_map/sum_cameras/pallas_call | solution.py:392
  52.4 0.0 copy-start.3
  52.4 0.0 copy-start.1
  52.4 0.0 copy-start.4
  52.5 0.0 copy-start.5
  52.5 17.2 %all_to_all.22 = f32[8,18,1,128]{3,2,1,0:T(1,128)S(1)} all-to-all(f32[8,18,1,128]{3,2,1,0:T(1,128)S(1)} %bitcast.24), channel_id=1, replica_groups=mesh['cam'=64,'pt'=8] {'pt'}, dimensions={0} | all-to-all | bytes 147456 | tf_op jit(solution)/shard_map/all_to_all | solution.py:433
  69.7 0.0 copy-done.3
  69.7 0.0 copy-done.1
  69.7 0.0 copy-done.4
  69.7 0.0 copy-done.5
  69.7 0.2 camera_scalars.1
  69.9 0.0 copy-start.6
  69.9 14.7 %all_to_all.23 = f32[64,1,1,128]{3,2,1,0:T(1,128)S(1)} all-to-all(f32[64,1,1,128]{3,2,1,0:T(1,128)S(1)} %bitcast.27), channel_id=1, replica_groups=mesh['cam'=64,'pt'=8] {'cam'}, dimensions={0} | all-to-all | bytes 65536 | tf_op jit(solution)/shard_map/all_to_all | solution.py:433
  84.6 0.0 copy-done.6
  84.6 0.7 update_vectors.1
  (1 shorter events, 0.0 us)
Async XLA Ops:
  2.2 29.2 %copy-start.7 = (f32[2048]{0:T(1024)S(1)}, f32[2048]{0:T(1024)}, u32[]{:S(2)}) copy-start(f32[2048]{0:T(1024)} %param.17) | copy-start | bytes 24580
  31.3 20.2 %copy-start = (f32[64,18,128]{2,0,1:T(8,128)S(1)}, f32[64,18,128]{2,0,1:T(8,128)}, u32[]{:S(2)}) copy-start(f32[64,18,128]{2,0,1:T(8,128)} %param.18) | copy-start | bytes 1769476
  34.8 16.7 %copy-start.2 = (s32[64,128]{1,0:T(8,128)S(1)}, s32[64,128]{1,0:T(8,128)}, u32[]{:S(2)}) copy-start(s32[64,128]{1,0:T(8,128)} %cam_ids.1) | copy-start | bytes 98308
  52.4 17.2 %copy-start.3 = (f32[81,256]{1,0:T(8,128)S(1)}, f32[81,256]{1,0:T(8,128)}, u32[]{:S(2)}) copy-start(f32[81,256]{1,0:T(8,128)} %precond.1) | copy-start | bytes 248836
  52.4 17.2 %copy-start.1 = (f32[9,256]{1,0:T(8,128)S(1)}, f32[9,256]{1,0:T(8,128)}, u32[]{:S(2)}) copy-start(f32[9,256]{1,0:T(8,128)} %direction.3) | copy-start | bytes 27652
  52.4 17.2 %copy-start.4 = (f32[9,256]{1,0:T(8,128)S(1)}, f32[9,256]{1,0:T(8,128)}, u32[]{:S(2)}) copy-start(f32[9,256]{1,0:T(8,128)} %residual.3) | copy-start | bytes 27652
  52.5 17.2 %copy-start.5 = (f32[9,256]{1,0:T(8,128)S(1)}, f32[9,256]{1,0:T(8,128)}, u32[]{:S(2)}) copy-start(f32[9,256]{1,0:T(8,128)} %damping.1) | copy-start | bytes 27652
  69.9 14.7 %copy-start.6 = (f32[9,256]{1,0:T(8,128)S(1)}, f32[9,256]{1,0:T(8,128)}, u32[]{:S(2)}) copy-start(f32[9,256]{1,0:T(8,128)} %solution_in.1) | copy-start | bytes 27652
